TPU v7x, 128 devices: a whole 4x4x4 slice. The times are simulated.
128 devices in a mesh: section: 4 (over x_lo, core), fsdp: 32 (over x_hi, z, y).
Axes of the slice: x: 4 (x_hi: 2, x_lo: 2; x = x_hi * 2 + x_lo), y: 4, z: 4, core: 2. Of those that a mesh axis runs over, the one named last changes fastest.
Arguments:
- saved_inputs: bfloat16 [4, 2, 32, 512, 1536], P('section', None, 'fsdp'), may hold values from -6 to 6
- grad_outputs: bfloat16 [2, 32, 512, 1536], P(None, 'fsdp'), may hold values from -6 to 6
- lengths: int32 [2, 32], P(None, 'fsdp'), may hold values from 256 to 512, as said below
- pointwise: bfloat16 [4, 1536, 1536], P('section', 'fsdp'), may hold values from -0.15625 to 0.15625
- depth_kernel: bfloat16 [4, 5, 1536], P('section', None, 'fsdp'), may hold values from -2.5 to 2.5
- norm_gain: bfloat16 [4, 1536], P('section', 'fsdp'), may hold values from 0.5 to 1.5
Outputs:
- frame_grads: bfloat16 [4, 2, 32, 512, 1536], P('section', None, 'fsdp')
- pointwise_grad: float32 [4, 1536, 1536], P('section', 'fsdp')
- kernel_grad: float32 [4, 5, 1536], P('section', None, 'fsdp')
- gain_grad: float32 [4, 1536], P('section', 'fsdp')
Inputs may be any that keep to these rules, and one draw needn't show every extreme that they name: `lengths`: frames at and after an utterance's length are padding; some utterance fills all 512 slots.
All inputs are finite; a program needn't handle non-finite values.
Results may differ from a plain program's by a relative error of at most 0.0057.
Values may be sent and summed in bfloat16 or wider, within the bound.
No kernel may reach another device: no remote copies, remote signals or barrier semaphores. Data moves between devices by JAX's collectives and lax.ppermute only.
A program may use at most 128 MiB of HBM per device.

v0:
```python
import jax
import jax.numpy as jnp
from jax import lax
from jax.sharding import PartitionSpec as P

EPSILON = 1e-05


def shifted(block, axis, distance):
    devices = range(lax.axis_size(axis))
    route = [(i - distance, i) for i in devices if i - distance in devices]
    return lax.ppermute(block, axis, route)


def depthwise(signal, kernel):
    tap_count = kernel.shape[0]
    margin = (tap_count - 1) // 2
    length = signal.shape[-2]
    widths = [(0, 0)] * (signal.ndim - 2) + [(margin, margin), (0, 0)]
    padded = jnp.pad(signal, widths)
    running = jnp.zeros(signal.shape, jnp.float32)
    for offset in range(tap_count):
        running = (
            running + kernel[offset].astype(jnp.float32) * padded[..., offset : offset + length, :]
        )
    return running


def tap_sums(upstream, signal, tap_count):
    margin = (tap_count - 1) // 2
    length = signal.shape[-2]
    widths = [(0, 0)] * (signal.ndim - 2) + [(margin, margin), (0, 0)]
    padded = jnp.pad(signal, widths)
    leading = tuple(range(signal.ndim - 1))
    return jnp.stack(
        [
            jnp.sum(upstream * padded[..., offset : offset + length, :], axis=leading)
            for offset in range(tap_count)
        ]
    )


def activation(inputs, present, kernel, gains):
    hidden = inputs.astype(jnp.float32) * present
    mixed = depthwise(hidden, kernel)
    average = jnp.mean(mixed, axis=-1, keepdims=True)
    centred = mixed - average
    inverse = lax.rsqrt(jnp.mean(centred * centred, axis=-1, keepdims=True) + EPSILON)
    normed = centred * inverse
    gained = normed * gains.astype(jnp.float32)
    logistic = jax.nn.sigmoid(gained)
    return (hidden, inverse, normed, gained, logistic)


def through_norm(
    grad_activated, hidden, inverse, normed, gained, logistic, kernel, gains, upstream, present
):
    grad_gained = grad_activated * (logistic + gained * logistic * (1.0 - logistic))
    leading = tuple(range(grad_gained.ndim - 1))
    gain_term = jnp.sum(grad_gained * normed, axis=leading)
    grad_normed = grad_gained * gains.astype(jnp.float32)
    grad_mixed = inverse * (
        grad_normed
        - jnp.mean(grad_normed, axis=-1, keepdims=True)
        - normed * jnp.mean(grad_normed * normed, axis=-1, keepdims=True)
    )
    kernel_term = tap_sums(grad_mixed, hidden, kernel.shape[0])
    grad_hidden = depthwise(grad_mixed, kernel[::-1])
    grad_inputs = (upstream + grad_hidden * present).astype(jnp.bfloat16)
    return (grad_inputs, kernel_term, gain_term)


def body(saved_inputs, grad_outputs, lengths, pointwise, depth_kernel, norm_gain):
    sections = lax.axis_size("section")
    section_id = lax.axis_index("section")
    local_inputs = saved_inputs[0, :, 0]
    local_grads = grad_outputs[:, 0]
    local_lengths = lengths[:, 0]
    micro_count, frames, features = local_inputs.shape
    factor = float(lax.axis_size("fsdp") * micro_count * frames) ** (-0.5)
    projection, kernel, gains = (
        lax.all_gather(pointwise[0], "fsdp", axis=0, tiled=True),
        lax.all_gather(depth_kernel[0], "fsdp", axis=1, tiled=True),
        lax.all_gather(norm_gain[0], "fsdp", axis=0, tiled=True),
    )
    places = jnp.arange(frames, dtype=jnp.int32)
    stores = (jnp.zeros((features, features), jnp.float32),)

    def compute_step(bundle):
        frame_out, kernel_sum, gain_sum, held, micro_slot, upstream_raw = bundle
        inputs = lax.dynamic_index_in_dim(local_inputs, micro_slot, 0, keepdims=False)
        length_now = lax.dynamic_index_in_dim(local_lengths, micro_slot, 0, keepdims=False)
        present = (places < length_now).astype(jnp.float32)[:, None]
        upstream = upstream_raw.astype(jnp.float32)
        hidden, inverse, normed, gained, logistic = activation(inputs, present, kernel, gains)
        activated = (gained * logistic).astype(jnp.bfloat16)
        grad_masked = (upstream * present).astype(jnp.bfloat16)
        grad_activated = lax.dot_general(
            grad_masked, projection, (((1,), (1,)), ((), ())), preferred_element_type=jnp.float32
        )
        grad_inputs, kernel_term, gain_term = through_norm(
            grad_activated,
            hidden,
            inverse,
            normed,
            gained,
            logistic,
            kernel,
            gains,
            upstream,
            present,
        )
        held = (
            held[0]
            + lax.dot_general(
                activated, grad_masked, (((0,), (0,)), ((), ())), preferred_element_type=jnp.float32
            ),
        )
        frame_out = lax.dynamic_update_index_in_dim(frame_out, grad_inputs, micro_slot, 0)
        return (grad_inputs, frame_out, kernel_sum + kernel_term, gain_sum + gain_term, held)

    def pass_step(bundle):
        frame_out, kernel_sum, gain_sum, held, micro_slot, upstream_raw = bundle
        return (jnp.zeros_like(upstream_raw), frame_out, kernel_sum, gain_sum, held)

    def one_turn(counter, loop_state):
        received, frame_out, kernel_sum, gain_sum, held = loop_state
        position = counter - (sections - 1 - section_id)
        active = jnp.logical_and(position >= 0, position < micro_count)
        micro_slot = jnp.clip(position, 0, micro_count - 1)
        outer_grad = lax.dynamic_index_in_dim(local_grads, micro_slot, 0, keepdims=False)
        upstream_raw = jnp.where(section_id == sections - 1, outer_grad, received)
        grad_inputs, frame_out, kernel_sum, gain_sum, held = lax.cond(
            active,
            compute_step,
            pass_step,
            (frame_out, kernel_sum, gain_sum, held, micro_slot, upstream_raw),
        )
        received = shifted(grad_inputs, "section", -1)
        return (received, frame_out, kernel_sum, gain_sum, held)

    initial = (
        jnp.zeros((frames, features), jnp.bfloat16),
        jnp.zeros((micro_count, frames, features), jnp.bfloat16),
        jnp.zeros(kernel.shape, jnp.float32),
        jnp.zeros((features,), jnp.float32),
        stores,
    )
    received, frame_out, kernel_sum, gain_sum, held = lax.fori_loop(
        0, micro_count + sections - 1, one_turn, initial
    )
    point_share, kernel_share, gain_share = (
        lax.psum_scatter(held[0], "fsdp", scatter_dimension=0, tiled=True),
        lax.psum_scatter(kernel_sum, "fsdp", scatter_dimension=1, tiled=True),
        lax.psum_scatter(gain_sum, "fsdp", scatter_dimension=0, tiled=True),
    )
    return (
        frame_out[None, :, None],
        (point_share * factor)[None],
        (kernel_share * factor)[None],
        (gain_share * factor)[None],
    )


def solution(mesh):
    placed = (
        P("section", None, "fsdp", None, None),
        P(None, "fsdp", None, None),
        P(None, "fsdp"),
        P("section", "fsdp", None),
        P("section", None, "fsdp"),
        P("section", "fsdp"),
    )
    return jax.shard_map(
        body,
        mesh=mesh,
        in_specs=placed,
        out_specs=(
            P("section", None, "fsdp", None, None),
            P("section", "fsdp", None),
            P("section", None, "fsdp"),
            P("section", "fsdp"),
        ),
        check_vma=False,
    )
```

profile of v0, /device:TPU:0, one launch (start us, length us, event | category | flops | bytes accessed | tf_op | source)
XLA Modules:
  0.0 916.9 jit_solution(1244989175964518420)
XLA Ops:
  8.8 102.0 %all-gather = bf16[1,5,1536]{1,0,2:T(2,128)(2,1)S(1)} all-gather(bf16[1,5,48]{1,0,2:T(2,128)(2,1)S(1)} %copy.13), channel_id=2, replica_groups=mesh['section'=4,'fsdp'=32] {'fsdp'}, dimensions={2}, use_global_device_ids=true | all-gather | bytes 15840 | tf_op jit(solution)/shard_map/all_gather | solution.py:83
  114.1 88.9 %all-reduce.2 = bf16[1536]{0:T(1024)(128)(2,1)S(1)} all-reduce(bf16[1536]{0:T(1024)(128)(2,1)S(1)} %dynamic-update-slice), channel_id=4, replica_groups=mesh['section'=4,'fsdp'=32] {'fsdp'}, use_global_device_ids=true, to_apply=%add.2 | all-reduce | flops 1536 | bytes 6144 | tf_op jit(solution)/shard_map/all_gather | solution.py:84
  205.1 4.8 broadcast_in_dim.42
  209.9 235.8 %while.24 = (s32[]{:T(128)}, bf16[512,1536]{1,0:T(8,128)(2,1)S(1)}, bf16[2,512,1536]{2,1,0:T(8,128)(2,1)}, f32[5,1536]{1,0:T(8,128)S(1)}, f32[1536]{0:T(1024)S(1...) while((s32[]{:T(128)}, bf16[512,1536]{1,0:T(8,128)(2,1)S(1)}, ...), condition=%wide.region_13.14_spmd.clone, body=%wide.region_0.13_spmd.clone.sunk | while | flops 4896336384 | bytes 110565944 | solution.py:149
  212.4 4.2 collective-permute-done
  219.2 19.4 %collective-permute-done = bf16[512,1536]{1,0:T(8,128)(2,1)S(1)} collective-permute-done((bf16[512,1536]{1,0:T(8,128)(2,1)}, bf16[512,1536]{1,0:T(8,128)(2,1)S(1)}, u32[]{:S(2)}, u32[]{:S(2)}) %collective-permute-start) | collective-permute-done | bytes 1572896 | tf_op jit(solution)/shard_map/while/body/eval_jaxpr/ppermute | solution.py:12
  241.2 96.7 %collective-permute-done = bf16[512,1536]{1,0:T(8,128)(2,1)S(1)} collective-permute-done((bf16[512,1536]{1,0:T(8,128)(2,1)}, bf16[512,1536]{1,0:T(8,128)(2,1)S(1)}, u32[]{:S(2)}, u32[]{:S(2)}) %collective-permute-start) | collective-permute-done | bytes 1572896 | tf_op jit(solution)/shard_map/while/body/eval_jaxpr/ppermute | solution.py:12
  337.9 40.2 %conditional.3 = (bf16[512,1536]{1,0:T(8,128)(2,1)}, bf16[2,512,1536]{2,1,0:T(8,128)(2,1)}, f32[5,1536]{1,0:T(8,128)S(1)}, f32[1536]{0:T(1024)S(1)}, f32[1536,1536]{1,0:T(8,128)}) conditional(s32[]{:T(128)} %convert_element_type.106, (bf16[2,512,1536]{2,1,0:T(8,128)(2,1)}, f32[5,1536]{1,0:T(8,128)S(1)}, f32[1536]{0:T(1024)S(1)}, ...), branch_computations={%region_1.1_spmd, %region_2.12_spmd} | conditional | flops 4896336384 | bytes 104272064 | solution.py:133
  343.1 2.4 fusion.16
  346.0 3.6 multiply_reduce_fusion
  349.7 8.5 multiply_reduce_fusion.1
  358.3 9.3 %bitcast_dynamic-update-slice_fusion = (bf16[2,512,1536]{2,1,0:T(8,128)(2,1)}, bf16[512,1536]{1,0:T(8,128)(2,1)}) fusion(bf16[2,512,1536]{2,1,0:T(8,128)(2,1)} %get-tuple-element.440, s32[]{:T(128)S(6)} %min.10, f32[512]{0:T(512)S(1)} %compare_convert_fusion, f32[1536]{0:T(1024)S(1)} %get-tuple-element.546, f32[1536]{0:T(1024)S(1)} %get-tuple-element.545, ...), kind=kLoop, calls=%fused_computation.28 | loop fusion | flops 10223616 | bytes 7897092 | tf_op jit(solution)/shard_map/while/body/eval_jaxpr/cond/branch_1_fun/jit(dynamic_update_index_in_dim)/dynamic_update_slice | solution.py:119
  367.6 10.5 %convolution_add_fusion = f32[1536,1536]{1,0:T(8,128)} fusion(f32[1536,1536]{1,0:T(8,128)} %get-tuple-element.443, f32[512,1536]{1,0:T(8,128)S(1)} %get-tuple-element.579, f32[1536]{0:T(1024)S(1)} %convert_element_type.78, f32[512]{0:T(512)S(1)} %add_rsqrt_fusion, f32[512]{0:T(512)S(1)} %broadcast_multiply_fusion.2, bf16[512,1536]{1,0:T(8,128)(2,1)S(1)} %copy-done.1, ...), kind=kOutput, calls=%fused_computation.1 | convolution fusion | flops 2426929152 | bytes 23605248 | tf_op jit(solution)/shard_map/while/body/eval_jaxpr/cond/branch_1_fun/dot_general | solution.py:115
  379.4 20.6 %collective-permute-done = bf16[512,1536]{1,0:T(8,128)(2,1)S(1)} collective-permute-done((bf16[512,1536]{1,0:T(8,128)(2,1)}, bf16[512,1536]{1,0:T(8,128)(2,1)S(1)}, u32[]{:S(2)}, u32[]{:S(2)}) %collective-permute-start) | collective-permute-done | bytes 1572896 | tf_op jit(solution)/shard_map/while/body/eval_jaxpr/ppermute | solution.py:12
  400.0 40.2 %conditional.3 = (bf16[512,1536]{1,0:T(8,128)(2,1)}, bf16[2,512,1536]{2,1,0:T(8,128)(2,1)}, f32[5,1536]{1,0:T(8,128)S(1)}, f32[1536]{0:T(1024)S(1)}, f32[1536,1536]{1,0:T(8,128)}) conditional(s32[]{:T(128)} %convert_element_type.106, (bf16[2,512,1536]{2,1,0:T(8,128)(2,1)}, f32[5,1536]{1,0:T(8,128)S(1)}, f32[1536]{0:T(1024)S(1)}, ...), branch_computations={%region_1.1_spmd, %region_2.12_spmd} | conditional | flops 4896336384 | bytes 104272064 | solution.py:133
  405.3 2.4 fusion.16
  408.2 3.6 multiply_reduce_fusion
  411.8 8.5 multiply_reduce_fusion.1
  420.5 9.3 %bitcast_dynamic-update-slice_fusion = (bf16[2,512,1536]{2,1,0:T(8,128)(2,1)}, bf16[512,1536]{1,0:T(8,128)(2,1)}) fusion(bf16[2,512,1536]{2,1,0:T(8,128)(2,1)} %get-tuple-element.440, s32[]{:T(128)S(6)} %min.10, f32[512]{0:T(512)S(1)} %compare_convert_fusion, f32[1536]{0:T(1024)S(1)} %get-tuple-element.546, f32[1536]{0:T(1024)S(1)} %get-tuple-element.545, ...), kind=kLoop, calls=%fused_computation.28 | loop fusion | flops 10223616 | bytes 7897092 | tf_op jit(solution)/shard_map/while/body/eval_jaxpr/cond/branch_1_fun/jit(dynamic_update_index_in_dim)/dynamic_update_slice | solution.py:119
  429.7 10.5 %convolution_add_fusion = f32[1536,1536]{1,0:T(8,128)} fusion(f32[1536,1536]{1,0:T(8,128)} %get-tuple-element.443, f32[512,1536]{1,0:T(8,128)S(1)} %get-tuple-element.579, f32[1536]{0:T(1024)S(1)} %convert_element_type.78, f32[512]{0:T(512)S(1)} %add_rsqrt_fusion, f32[512]{0:T(512)S(1)} %broadcast_multiply_fusion.2, bf16[512,1536]{1,0:T(8,128)(2,1)S(1)} %copy-done.1, ...), kind=kOutput, calls=%fused_computation.1 | convolution fusion | flops 2426929152 | bytes 23605248 | tf_op jit(solution)/shard_map/while/body/eval_jaxpr/cond/branch_1_fun/dot_general | solution.py:115
  441.5 4.2 collective-permute-done
  448.3 92.5 %all-reduce.3 = f32[1536]{0:T(1024)S(1)} all-reduce(f32[1536]{0:T(1024)S(1)} %get-tuple-element.476), channel_id=7, replica_groups=mesh['section'=4,'fsdp'=32] {'fsdp'}, use_global_device_ids=true, to_apply=%region_16.17.clone | all-reduce | flops 1536 | bytes 12288
  541.5 122.3 %reduce-scatter.7.cloned.1.call-done = f32[48,5]{1,0:T(8,128)} async-done(((f32[1536,5]{1,0:T(8,128)}), f32[48,5]{1,0:T(8,128)}) %reduce-scatter.7.cloned.1.call-update) | async-done | bytes 976
  665.2 243.5 %reduce-scatter.5.cloned.1.call-done = f32[48,1536]{1,0:T(8,128)} async-done(((f32[1536,1536]{1,0:T(8,128)}), f32[48,1536]{1,0:T(8,128)}) %reduce-scatter.5.cloned.1.call-update) | async-done | bytes 294928 | tf_op jit(solution)/shard_map/reduce_scatter | solution.py:153
  (94 shorter events, 37.4 us)
Async XLA Ops:
  7.2 195.9 %all-gather.5.cloned.1.call-start = ((), (), s32[]{:S(2)}) async-start(), calls=%async_computation.3 | async-start | bytes 4866048 | tf_op jit(solution)/shard_map/all_gather | solution.py:82
  7.9 655.9 %reduce-scatter.7.cloned.1.call-start = ((), (), s32[]{:S(2)}) async-start(), calls=%async_computation.4 | async-start | bytes 811008
  205.1 4.8 copy-start.2
  211.1 5.5 collective-permute-start
  217.9 20.7 %collective-permute-start = (bf16[512,1536]{1,0:T(8,128)(2,1)}, bf16[512,1536]{1,0:T(8,128)(2,1)S(1)}, u32[]{:S(2)}, u32[]{:S(2)}) collective-permute-start(bf16[512,1536]{1,0:T(8,128)(2,1)} %get-tuple-element.675), channel_id=1, source_target_pairs={{32,0},{64,32},{96,64},{33,1},{65,33},{97,65},{34,2},{66,34},{98,6... | collective-permute-start | bytes 4718600 | tf_op jit(solution)/shard_map/while/body/eval_jaxpr/ppermute | solution.py:12
  239.9 98.0 %collective-permute-start = (bf16[512,1536]{1,0:T(8,128)(2,1)}, bf16[512,1536]{1,0:T(8,128)(2,1)S(1)}, u32[]{:S(2)}, u32[]{:S(2)}) collective-permute-start(bf16[512,1536]{1,0:T(8,128)(2,1)} %get-tuple-element.675), channel_id=1, source_target_pairs={{32,0},{64,32},{96,64},{33,1},{65,33},{97,65},{34,2},{66,34},{98,6... | collective-permute-start | bytes 4718600 | tf_op jit(solution)/shard_map/while/body/eval_jaxpr/ppermute | solution.py:12
  340.8 5.2 copy-start
  340.8 5.2 slice-start
  343.1 2.9 slice-start.1
  358.3 9.3 %copy-start.1 = (bf16[512,1536]{1,0:T(8,128)(2,1)S(1)}, bf16[512,1536]{1,0:T(8,128)(2,1)}, u32[]{:S(2)}) copy-start(bf16[512,1536]{1,0:T(8,128)(2,1)} %copy-done) | copy-start | bytes 4718596 | tf_op jit(solution)/shard_map/while/body/eval_jaxpr/cond
  378.1 21.9 %collective-permute-start = (bf16[512,1536]{1,0:T(8,128)(2,1)}, bf16[512,1536]{1,0:T(8,128)(2,1)S(1)}, u32[]{:S(2)}, u32[]{:S(2)}) collective-permute-start(bf16[512,1536]{1,0:T(8,128)(2,1)} %get-tuple-element.675), channel_id=1, source_target_pairs={{32,0},{64,32},{96,64},{33,1},{65,33},{97,65},{34,2},{66,34},{98,6... | collective-permute-start | bytes 4718600 | tf_op jit(solution)/shard_map/while/body/eval_jaxpr/ppermute | solution.py:12
  403.0 5.2 copy-start
  403.0 5.2 slice-start
  405.3 2.9 slice-start.1
  420.4 9.3 %copy-start.1 = (bf16[512,1536]{1,0:T(8,128)(2,1)S(1)}, bf16[512,1536]{1,0:T(8,128)(2,1)}, u32[]{:S(2)}) copy-start(bf16[512,1536]{1,0:T(8,128)(2,1)} %copy-done) | copy-start | bytes 4718596 | tf_op jit(solution)/shard_map/while/body/eval_jaxpr/cond
  440.2 5.5 collective-permute-start
  446.9 461.8 %reduce-scatter.5.cloned.1.call-start = ((), (), s32[]{:S(2)}) async-start(), calls=%async_computation.2 | async-start | bytes 9732096 | tf_op jit(solution)/shard_map/reduce_scatter | solution.py:153
Sparse Core Ops, SparseCore 0:
  11.0 86.2 all-gather.4
  447.0 216.7 reduce-scatter.6
  669.9 238.7 reduce-scatter.4
where the time goes:
time: 918 us; the launch traced here: 917 us
  waiting for transfers between devices  512 us (56%)
  blocking collectives  283 us (31%)
  other arithmetic  52.8 us (6%)
  matrix products  28.2 us (3%)
  local copies, waits for them, and re-layouts  18.1 us (2%)
  between operations  15.2 us (2%)
    reduce_scatter x1, waiting for transfers between devices, body(): lax.psum_scatter(held[0], 'fsdp', scatter_dimension=0, tiled=True)  243 us
    ppermute x5, waiting for transfers between devices, shifted(): return lax.ppermute(block, axis, route)  145 us
    unnamed x4, waiting for transfers between devices  124 us
    all_gather x1, blocking collectives, body(): lax.all_gather(depth_kernel[0], 'fsdp', axis=1, tiled=True)  102 us
    unnamed x1, blocking collectives  92.5 us
    all_gather x1, blocking collectives, body(): lax.all_gather(norm_gain[0], 'fsdp', axis=0, tiled=True)  88.9 us
    dot_general x2, matrix products, compute_step(): lax.dot_general(activated, grad_masked, (((0,), (0,)), ((), ())), preferr...  20.9 us
    dynamic_update_slice x2, other arithmetic, compute_step(): lax.dynamic_update_index_in_dim(frame_out, grad_inputs, micro_slot, 0)  18.5 us
  transfers between devices with their start and end apart: 8, of which 7 were waited for; matrix products, arithmetic and copies ran while one was open for 1% of the time, Pallas kernels for 0%

commit v1 on v0

v1 whole, which is shorter than its diff:
```python
import functools

import jax
import jax.numpy as jnp
import numpy as np
from jax import lax
from jax.experimental import pallas as pl
from jax.experimental.pallas import tpu as pltpu
from jax.sharding import Mesh
from jax.sharding import PartitionSpec as P

EPSILON = 1e-05
F32 = jnp.float32
BF16 = jnp.bfloat16
LANES = 128
PAD = 8
ANY = pl.BlockSpec(memory_space=pl.ANY)
SMEM = pl.BlockSpec(memory_space=pltpu.SMEM)
VMEM = pl.BlockSpec(memory_space=pltpu.VMEM)

GATHERED = [(0, 0), (0, 1), (3, 0), (3, 1), (1, 0), (1, 1), (2, 0), (2, 1)]
SCATTERED = [(2, 0), (1, 1), (2, 1), (3, 0), (1, 0), (3, 1), (0, 0), (0, 1)]


def params(limit, **kw):
    return pltpu.CompilerParams(vmem_limit_bytes=limit << 20, **kw)


def cost(us):
    return pl.CostEstimate(flops=int(us * 1.0e9), bytes_accessed=1 << 20, transcendentals=0)


def tables():
    gather = np.zeros((2, 4, 4, 2, 5, 8), np.int32)
    scatter = np.zeros((2, 4, 4, 2, 32), np.int32)
    for x in range(2):
        for z in range(4):
            for y in range(4):
                for half in range(2):
                    inner, outer = (y, z) if half == 0 else (z, y)

                    def block(o, i, r):
                        a, b, c = (outer + o) % 4, (inner + i) % 4, (x + r) % 2
                        zz, yy = (a, b) if half == 0 else (b, a)
                        return c * 16 + zz * 4 + yy

                    for slot, o in enumerate((0, 3, 1, 2)):
                        for j, (i, r) in enumerate(GATHERED):
                            gather[x, z, y, half, slot, j] = block(o, i, r)
                    for o in range(4):
                        for j, (i, r) in enumerate(SCATTERED):
                            base = {2: (0, 8), 1: (16, 4), 3: (12, 20), 0: (24, 28)}[o]
                            place = base[0] + j if j < 4 else base[1] + j - 4
                            scatter[x, z, y, half, block(o, i, r)] = place
    return gather.reshape(2, 4, 4, -1), scatter.reshape(2, 4, 4, -1)


def forward_kernel(lens, x_ref, taps, normed_ref, slope_ref, inv_ref, act_ref, hid, mix):
    m = pl.program_id(0)
    length = lens[m]
    frames, feats = x_ref.shape[1:]
    cols = feats // LANES
    for c in range(cols):
        hid[c, 0:PAD, :] = jnp.zeros((PAD, LANES), F32)
        hid[c, PAD + frames : 2 * PAD + frames, :] = jnp.zeros((PAD, LANES), F32)

    def load(i, carry):
        r = pl.multiple_of(i * 16, 16)
        rows = r + lax.broadcasted_iota(jnp.int32, (16, LANES), 0)
        keep = rows < length
        for c in range(cols):
            v = x_ref[0, pl.ds(r, 16), c * LANES : (c + 1) * LANES].astype(F32)
            hid[c, pl.ds(r + PAD, 16), :] = jnp.where(keep, v, 0.0)
        return carry

    lax.fori_loop(0, frames // 16, load, 0)
    for c in range(cols):
        span = slice(c * LANES, (c + 1) * LANES)
        weights = [jnp.broadcast_to(taps[k : k + 1, span], (64, LANES)) for k in range(5)]

        def conv(i, carry):
            r = pl.multiple_of(i * 64, 64)
            total = weights[0] * hid[c, pl.ds(r + PAD - 2, 64), :]
            for k in range(1, 5):
                total = total + weights[k] * hid[c, pl.ds(r + PAD - 2 + k, 64), :]
            mix[pl.ds(r, 64), span] = total
            return carry

        lax.fori_loop(0, frames // 64, conv, 0)

    def norm(i, carry):
        r = pl.multiple_of(i * 16, 16)
        mixed = mix[pl.ds(r, 16), :]
        centred = mixed - jnp.mean(mixed, axis=-1, keepdims=True)
        inverse = lax.rsqrt(jnp.mean(centred * centred, axis=-1, keepdims=True) + EPSILON)
        gain = taps[5:6, :]
        normed = centred * inverse
        gained = normed * gain
        logistic = jax.nn.sigmoid(gained)
        normed_ref[0, pl.ds(r, 16), :] = normed.astype(BF16)
        slope_ref[0, pl.ds(r, 16), :] = (
            (logistic + gained * logistic * (1.0 - logistic)) * gain
        ).astype(BF16)
        act_ref[0, pl.ds(r, 16), :] = (gained * logistic).astype(BF16)
        inv_ref[0, pl.ds(r, 16), :] = jnp.broadcast_to(inverse, (16, LANES))
        return carry

    lax.fori_loop(0, frames // 16, norm, 0, unroll=2)


def forward(lens, x, taps):
    micro, frames, feats = x.shape
    block = pl.BlockSpec((1, frames, feats), lambda m: (m, 0, 0))
    return pl.pallas_call(
        forward_kernel,
        grid=(micro,),
        in_specs=[SMEM, block, pl.BlockSpec(taps.shape, lambda m: (0, 0))],
        out_specs=[block, block, pl.BlockSpec((1, frames, LANES), lambda m: (m, 0, 0)), block],
        out_shape=[
            jax.ShapeDtypeStruct(x.shape, BF16),
            jax.ShapeDtypeStruct(x.shape, BF16),
            jax.ShapeDtypeStruct((micro, frames, LANES), F32),
            jax.ShapeDtypeStruct(x.shape, BF16),
        ],
        scratch_shapes=[
            pltpu.VMEM((feats // LANES, frames + 2 * PAD, LANES), F32),
            pltpu.VMEM((frames, feats), F32),
        ],
        compiler_params=params(40),
        cost_estimate=cost(12),
    )(lens, x, taps)


def relay_kernel(first, step, grads, come, *rest):
    (wa, wb), rest = (rest[:5], rest[5:10]), rest[10:]
    normed_in, slope_in, inv_in, taps, rest = *rest[:4], rest[4:]
    if not first:
        rest = rest[4:]
    send, frame_out, masked_out, mixed_out, gain_out = rest[:5]
    w, up, gm, normed, slope, inv, ga, gmix, out, gsum, sems = rest[5:]
    frames, feats = up.shape
    cols = feats // LANES
    half = feats // 2
    rows = 48
    active, slot, last, length = step[0], step[1], step[2], step[3]

    def pieces():
        made = []
        for h, parts in enumerate((wa, wb)):
            for p in range(5):
                for j in range(parts[p].shape[0]):
                    at = h * 40 + (p * 8 + j if p < 4 else 28 + j)
                    place = pl.multiple_of(step[8 + at] * rows, 16)
                    made.append(
                        pltpu.make_async_copy(
                            parts[p].at[j],
                            w.at[pl.ds(place, rows), pl.ds(h * half, half)],
                            sems.at[0],
                        )
                    )
        return made

    @pl.when(active == 1)
    def _():
        @pl.when(last == 1)
        def _():
            pltpu.make_async_copy(grads.at[slot], up, sems.at[1]).start()

        @pl.when(last == 0)
        def _():
            pltpu.make_async_copy(come, up, sems.at[1]).start()

        weights = pieces()
        for copy in weights:
            copy.start()
        others = [
            pltpu.make_async_copy(normed_in.at[slot], normed, sems.at[2]),
            pltpu.make_async_copy(slope_in.at[slot], slope, sems.at[3]),
            pltpu.make_async_copy(inv_in.at[slot], inv, sems.at[4]),
        ]
        for copy in others:
            copy.start()
        for c in range(cols):
            gmix[c, 0:PAD, :] = jnp.zeros((PAD, LANES), F32)
            gmix[c, PAD + frames : 2 * PAD + frames, :] = jnp.zeros((PAD, LANES), F32)
        pltpu.make_async_copy(come, up, sems.at[1]).wait()

        def mask(i, carry):
            r = pl.multiple_of(i * 16, 16)
            keep = r + lax.broadcasted_iota(jnp.int32, (16, feats), 0) < length
            v = up[pl.ds(r, 16), :].astype(F32)
            gm[pl.ds(r, 16), :] = jnp.where(keep, v, 0.0).astype(BF16)
            return carry

        lax.fori_loop(0, frames // 16, mask, 0)
        masked_copy = pltpu.make_async_copy(gm, masked_out.at[slot], sems.at[5])
        masked_copy.start()
        for copy in weights:
            copy.wait()

        def multiply(n, carry):
            r = pl.multiple_of(n * 256, 256)
            ga[:, pl.ds(r, 256)] = lax.dot_general(
                gm[...], w[pl.ds(r, 256), :], (((1,), (1,)), ((), ())), preferred_element_type=F32
            )
            return carry

        lax.fori_loop(0, feats // 256, multiply, 0)
        for copy in others:
            copy.wait()
        gsum[...] = jnp.zeros_like(gsum)

        def through(i, carry):
            r = pl.multiple_of(i * 16, 16)
            gn = ga[pl.ds(r, 16), :] * slope[pl.ds(r, 16), :].astype(F32)
            nm = normed[pl.ds(r, 16), :].astype(F32)
            both = gn * nm
            gsum[...] += both[:8] + both[8:]
            a = jnp.sum(gn, axis=-1, keepdims=True) * (1.0 / feats)
            b = jnp.sum(both, axis=-1, keepdims=True) * (1.0 / feats)
            mixed = inv[pl.ds(r, 16), 0:1] * (gn - a - nm * b)
            for c in range(cols):
                gmix[c, pl.ds(r + PAD, 16), :] = mixed[:, c * LANES : (c + 1) * LANES]
            return carry

        lax.fori_loop(0, frames // 16, through, 0, unroll=2)
        saved = [
            pltpu.make_async_copy(gmix, mixed_out.at[slot], sems.at[6]),
            pltpu.make_async_copy(gsum, gain_out.at[slot], sems.at[7]),
        ]
        for copy in saved:
            copy.start()
        for c in range(cols):
            span = slice(c * LANES, (c + 1) * LANES)
            kernel = [jnp.broadcast_to(taps[k : k + 1, span], (64, LANES)) for k in range(5)]

            def conv(i, carry):
                r = pl.multiple_of(i * 64, 64)
                total = kernel[4] * gmix[c, pl.ds(r + PAD - 2, 64), :]
                for k in range(1, 5):
                    total = total + kernel[4 - k] * gmix[c, pl.ds(r + PAD - 2 + k, 64), :]
                keep = r + lax.broadcasted_iota(jnp.int32, (64, LANES), 0) < length
                result = up[pl.ds(r, 64), span].astype(F32) + jnp.where(keep, total, 0.0)
                out[pl.ds(r, 64), span] = result.astype(BF16)
                return carry

            lax.fori_loop(0, frames // 64, conv, 0)
        ends = [
            pltpu.make_async_copy(out, send, sems.at[8]),
            pltpu.make_async_copy(out, frame_out.at[slot], sems.at[9]),
        ]
        for copy in ends:
            copy.start()
        for copy in [masked_copy] + saved + ends:
            copy.wait()


def relay(step, grads, come, weights, saved, taps, state):
    micro, frames, feats = grads.shape
    cols = feats // LANES
    first = state is None
    shapes = [
        jax.ShapeDtypeStruct((frames, feats), BF16),
        jax.ShapeDtypeStruct((micro, frames, feats), BF16),
        jax.ShapeDtypeStruct((micro, frames, feats), BF16),
        jax.ShapeDtypeStruct((micro, cols, frames + 2 * PAD, LANES), F32),
        jax.ShapeDtypeStruct((micro, 8, feats), F32),
    ]
    operands = [step, grads, come, *weights, *saved, taps]
    specs = [SMEM] + [ANY] * (len(operands) - 2) + [VMEM]
    aliases = {}
    if not first:
        aliases = {len(operands) + i: 1 + i for i in range(4)}
        operands += list(state)
        specs += [ANY] * 4
    out = pl.pallas_call(
        functools.partial(relay_kernel, first),
        in_specs=specs,
        out_specs=[ANY] * 5,
        out_shape=shapes,
        input_output_aliases=aliases,
        scratch_shapes=[
            pltpu.VMEM((feats, feats), BF16),
            pltpu.VMEM((frames, feats), BF16),
            pltpu.VMEM((frames, feats), BF16),
            pltpu.VMEM((frames, feats), BF16),
            pltpu.VMEM((frames, feats), BF16),
            pltpu.VMEM((frames, LANES), F32),
            pltpu.VMEM((frames, feats), F32),
            pltpu.VMEM((cols, frames + 2 * PAD, LANES), F32),
            pltpu.VMEM((frames, feats), BF16),
            pltpu.VMEM((8, feats), F32),
            pltpu.SemaphoreType.DMA((10,)),
        ],
        compiler_params=params(40),
        cost_estimate=cost(8),
    )(*operands)
    return out[0], tuple(out[1:])


def weight_kernel(step, act_in, masked_in, come, *rest):
    outs, (act, gm, acc, block, sems) = rest[:6], rest[6:]
    frames = come.shape[0]
    feats = come.shape[1]
    half = feats // 2
    head, length = step[0], step[1]
    copies = [
        pltpu.make_async_copy(act_in.at[0], act.at[pl.ds(0, frames)], sems.at[0]),
        pltpu.make_async_copy(act_in.at[1], act.at[pl.ds(frames, frames)], sems.at[1]),
        pltpu.make_async_copy(masked_in.at[0], gm.at[pl.ds(0, frames)], sems.at[2]),
    ]
    for copy in copies:
        copy.start()

    @pl.when(head == 1)
    def _():
        pltpu.make_async_copy(come, gm.at[pl.ds(frames, frames)], sems.at[3]).start()

    @pl.when(head == 0)
    def _():
        pltpu.make_async_copy(masked_in.at[1], gm.at[pl.ds(frames, frames)], sems.at[3]).start()

    pltpu.make_async_copy(come, gm.at[pl.ds(frames, frames)], sems.at[3]).wait()

    def mask(i, carry):
        r = pl.multiple_of(i * 16, 16)
        keep = r + lax.broadcasted_iota(jnp.int32, (16, feats), 0) < length
        v = gm[pl.ds(r + frames, 16), :].astype(F32)
        gm[pl.ds(r + frames, 16), :] = jnp.where(keep, v, 0.0).astype(BF16)
        return carry

    lax.fori_loop(0, frames // 16, mask, 0)
    for copy in copies:
        copy.wait()
    leaving = []
    for h in range(2):

        def multiply(n, carry):
            r = pl.multiple_of(n * 256, 256)
            acc[pl.ds(r, 256), :] = lax.dot_general(
                act[:, pl.ds(r, 256)],
                gm[:, h * half : (h + 1) * half],
                (((0,), (0,)), ((), ())),
                preferred_element_type=F32,
            )
            return carry

        lax.fori_loop(0, feats // 256, multiply, 0)

        def place(b, carry):
            r = pl.multiple_of(b * 48, 16)
            block[h, step[8 + h * 32 + b]] = acc[pl.ds(r, 48), :].astype(BF16)
            return carry

        lax.fori_loop(0, 32, place, 0)
        for p, (start, size) in enumerate(((0, 8), (8, 8), (16, 16))):
            copy = pltpu.make_async_copy(
                block.at[h, pl.ds(start, size)], outs[h * 3 + p], sems.at[4 + h * 3 + p]
            )
            copy.start()
            leaving.append(copy)
    for copy in leaving:
        copy.wait()


def weight_terms(step, act, masked, come):
    frames, feats = come.shape
    half = feats // 2
    sizes = (8, 8, 16)
    return pl.pallas_call(
        weight_kernel,
        in_specs=[SMEM, ANY, ANY, ANY],
        out_specs=[ANY] * 6,
        out_shape=[jax.ShapeDtypeStruct((n, 48, half), BF16) for n in sizes] * 2,
        scratch_shapes=[
            pltpu.VMEM((2 * frames, feats), BF16),
            pltpu.VMEM((2 * frames, feats), BF16),
            pltpu.VMEM((feats, half), F32),
            pltpu.VMEM((2, 32, 48, half), BF16),
            pltpu.SemaphoreType.DMA((10,)),
        ],
        compiler_params=params(40),
        cost_estimate=cost(8),
    )(step, act, masked, come)


def tap_kernel(lens, x_ref, mixed_ref, gain_ref, taps, out, hid):
    m = pl.program_id(0)
    length = lens[m]
    frames, feats = x_ref.shape[1:]
    cols = feats // LANES

    @pl.when(m == 0)
    def _():
        out[...] = jnp.zeros_like(out)

    for c in range(cols):
        hid[c, 0:PAD, :] = jnp.zeros((PAD, LANES), F32)
        hid[c, PAD + frames : 2 * PAD + frames, :] = jnp.zeros((PAD, LANES), F32)

    def load(i, carry):
        r = pl.multiple_of(i * 16, 16)
        keep = r + lax.broadcasted_iota(jnp.int32, (16, LANES), 0) < length
        for c in range(cols):
            v = x_ref[0, pl.ds(r, 16), c * LANES : (c + 1) * LANES].astype(F32)
            hid[c, pl.ds(r + PAD, 16), :] = jnp.where(keep, v, 0.0)
        return carry

    lax.fori_loop(0, frames // 16, load, 0)
    for c in range(cols):
        span = slice(c * LANES, (c + 1) * LANES)

        def add(i, sums):
            r = pl.multiple_of(i * 32, 32)
            grown = list(sums)
            for q in range(4):
                g = mixed_ref[0, c, pl.ds(r + PAD + 8 * q, 8), :]
                for k in range(5):
                    grown[k] = grown[k] + g * hid[c, pl.ds(r + PAD - 2 + k + 8 * q, 8), :]
            return tuple(grown)

        sums = lax.fori_loop(0, frames // 32, add, (jnp.zeros((8, LANES), F32),) * 5)
        for k in range(5):
            out[k : k + 1, span] += jnp.sum(sums[k], axis=0, keepdims=True)
    out[5:6, :] += jnp.sum(gain_ref[0], axis=0, keepdims=True) / taps[5:6, :]


def tap_terms(lens, x, mixed, gain, taps):
    micro, frames, feats = x.shape
    return pl.pallas_call(
        tap_kernel,
        grid=(micro,),
        in_specs=[
            SMEM,
            pl.BlockSpec((1, frames, feats), lambda m: (m, 0, 0)),
            pl.BlockSpec((1,) + mixed.shape[1:], lambda m: (m, 0, 0, 0)),
            pl.BlockSpec((1, 8, feats), lambda m: (m, 0, 0)),
            pl.BlockSpec(taps.shape, lambda m: (0, 0)),
        ],
        out_specs=pl.BlockSpec((8, feats), lambda m: (0, 0)),
        out_shape=jax.ShapeDtypeStruct((8, feats), F32),
        scratch_shapes=[pltpu.VMEM((feats // LANES, frames + 2 * PAD, LANES), F32)],
        compiler_params=params(40),
        cost_estimate=cost(8),
    )(lens, x, mixed, gain, taps)


def shift(x, axis, d):
    n = lax.axis_size(axis)
    return lax.ppermute(x, axis, [(i, (i + d) % n) for i in range(n)])


def swap(x, axis, d):
    n = lax.axis_size(axis)
    return lax.ppermute(x, axis, [(i, i ^ d) for i in range(n)])


def gather_weights(shard):
    half = shard.shape[1] // 2
    other = swap(shard, "xh", 1)
    pairs = [
        jnp.stack([shard[:, :half], other[:, :half]]),
        jnp.stack([shard[:, half:], other[:, half:]]),
    ]

    def ring(own, axis):
        cut = own.shape[0] // 2
        left, right = shift(own, axis, 1), shift(own, axis, -1)
        return own, left, right, shift(left[:cut], axis, 1), shift(right[cut:], axis, -1)

    first = [jnp.concatenate(ring(p, a)) for p, a in zip(pairs, ("y", "z"))]
    return [ring(p, a) for p, a in zip(first, ("z", "y"))]


def sum_everywhere(x):
    for axis, d in (("xh", 1), ("z", 1), ("z", 2), ("y", 1), ("y", 2)):
        x = x + swap(x, axis, d)
    return x


def scatter_ring(plus, minus, kept, axis):
    n = plus.shape[0] // 2
    up_a, dn_b, own_a, own_b = (kept[i * n : (i + 1) * n].astype(F32) for i in range(4))
    p, q = shift(plus, axis, 1), shift(minus, axis, -1)
    far_p = shift((up_a + p[:n].astype(F32)).astype(BF16), axis, 1)
    far_q = shift((dn_b + q[:n].astype(F32)).astype(BF16), axis, -1)
    a = own_a + far_p.astype(F32) + q[n:].astype(F32)
    b = own_b + far_q.astype(F32) + p[n:].astype(F32)
    return a, b


def scatter_weights(parts):
    first = [scatter_ring(*parts[:3], "z"), scatter_ring(*parts[3:], "y")]
    second = []
    for (a, b), axis in zip(first, ("y", "z")):
        a, b = a.astype(BF16), b.astype(BF16)
        second.append(scatter_ring(a[:2], a[2:], b, axis))
    own = jnp.concatenate([a[0] for a, _ in second], axis=1)
    give = jnp.concatenate([b[0] for _, b in second], axis=1).astype(BF16)
    return own + swap(give, "xh", 1).astype(F32)


def body(saved_inputs, grad_outputs, lengths, pointwise, depth_kernel, norm_gain):
    section = lax.axis_index("section")
    x, z, y = (lax.axis_index(a) for a in ("xh", "z", "y"))
    inputs = saved_inputs[0, :, 0]
    grads = grad_outputs[:, 0]
    lens = lengths[:, 0]
    micro, frames, features = inputs.shape
    factor = float(32 * micro * frames) ** (-0.5)
    place = (x * 16 + z * 4 + y) * 48

    small = jnp.concatenate([depth_kernel[0], norm_gain[0:1]], axis=0)
    small = lax.dynamic_update_slice(jnp.zeros((6, features), BF16), small, (0, place))
    taps = jnp.pad(sum_everywhere(small).astype(F32), ((0, 2), (0, 0)))
    halves = gather_weights(pointwise[0])
    weights = [*halves[0], *halves[1]]
    normed, slope, inverse, act = forward(lens, inputs, taps)

    gather_table, scatter_table = tables()
    gather_at = jnp.asarray(gather_table)[x, z, y]
    scatter_at = jnp.asarray(scatter_table)[x, z, y]

    def turn(state, come, who):
        slot = jnp.asarray(who, jnp.int32)[section]
        at = jnp.maximum(slot, 0)
        flags = [slot >= 0, at, section == 3, lens[at], 0, 0, 0, 0]
        step = jnp.concatenate([jnp.stack([jnp.asarray(f, jnp.int32) for f in flags]), gather_at])
        return relay(step, grads, come, weights, (normed, slope, inverse), taps, state)

    def hop(block, route):
        return lax.ppermute(block, "section", route)

    sent, state = turn(None, grads[0], (-1, -1, -1, 0))
    come = hop(sent, [(3, 2)])
    sent, state = turn(state, come, (-1, -1, 0, 1))
    come = hop(sent, [(3, 2), (2, 1), (1, 0)])
    sent, state = turn(state, come, (-1, 0, 1, -1))
    come = hop(sent, [(3, 2), (2, 1), (1, 0)])
    sent, state = turn(state, come, (0, 1, -1, -1))
    come = hop(sent, [(1, 0)])
    head = section == 0
    flags = [head, lens[1], 0, 0, 0, 0, 0, 0]
    step = jnp.concatenate([jnp.stack([jnp.asarray(f, jnp.int32) for f in flags]), scatter_at])
    parts = weight_terms(step, act, state[1], come)
    point_share = scatter_weights(parts)
    sent, state = turn(state, come, (1, -1, -1, -1))
    frame_out, _, mixed, gain = state
    terms = sum_everywhere(tap_terms(lens, inputs, mixed, gain, taps))
    share = lax.dynamic_slice(terms, (0, place), (8, 48)) * factor
    return (
        frame_out[None, :, None],
        (point_share * factor)[None],
        share[None, :5],
        share[5:6],
    )


def solution(mesh):
    fine = Mesh(mesh.devices.reshape(4, 2, 4, 4), ("section", "xh", "z", "y"))
    fsdp = ("xh", "z", "y")
    return jax.shard_map(
        body,
        mesh=fine,
        in_specs=(
            P("section", None, fsdp, None, None),
            P(None, fsdp, None, None),
            P(None, fsdp),
            P("section", fsdp, None),
            P("section", None, fsdp),
            P("section", fsdp),
        ),
        out_specs=(
            P("section", None, fsdp, None, None),
            P("section", fsdp, None),
            P("section", None, fsdp),
            P("section", fsdp),
        ),
        check_vma=False,
    )
```

time: 918 us -> 311 us (0.34)
  waiting for transfers between devices: 512 us -> 117 us
  blocking collectives: 283 us -> 0 us
  starting transfers between devices: 6.52 us -> 66.5 us
  Pallas kernels: 0 us -> 58 us
  other arithmetic: 52.8 us -> 3.36 us
  local copies, waits for them, and re-layouts: 18.1 us -> 55.3 us
  matrix products: 28.2 us -> 0 us
    reduce_scatter x1 -> x0, waiting for transfers between devices: 243 us -> none  [body(): lax.psum_scatter(held[0], 'fsdp', scatter_dimension=0, tiled=True)]
    all_gather x2 -> x0, blocking collectives: 191 us -> none  [the longest x1 102 us: body(): lax.all_gather(depth_kernel[0], 'fsdp', axis=1, tiled=True)]
    unnamed x4 -> x0, waiting for transfers between devices: 124 us -> none
    unnamed x1 -> x0, blocking collectives: 92.5 us -> none
    ppermute x5 -> x48, starting transfers between devices: 6.4 us -> 66.5 us  [the longest x32 42.1 us: shift(): return lax.ppermute(x, axis, [(i, (i + d) % n) for i in range(n)])]
    pallas_call x0 -> x8, Pallas kernels: none -> 58 us  [the longest x5 27.6 us: relay(): pl.pallas_call(functools.partial(relay_kernel, first), in_specs=specs, ou...]
    unnamed x9 -> x95, local copies, waits for them, and re-layouts: 5.65 us -> 41.9 us
    dot_general x4 -> x0, matrix products: 28.2 us -> none  [the longest x2 20.9 us: compute_step(): lax.dot_general(activated, grad_masked, (((0,), (0,)), ((), ())), preferr...]
  transfers between devices with their start and end apart: 8 -> 48, of which waited for: 7 -> 21; matrix products, arithmetic and copies ran while one was open for 1% -> 7% of each run, Pallas kernels for 0% -> 10%
where the time goes in v1:
time: 311 us; the launch traced here: 308 us
  waiting for transfers between devices  117 us (38%)
  starting transfers between devices  66.5 us (21%)
  Pallas kernels  58 us (19%)
  local copies, waits for them, and re-layouts  55.3 us (18%)
  between operations  7.89 us (3%)
  other arithmetic  3.36 us (1%)
    ppermute x4, waiting for transfers between devices, hop(): return lax.ppermute(block, 'section', route)  67.9 us
    ppermute x32, starting transfers between devices, shift(): return lax.ppermute(x, axis, [(i, (i + d) % n) for i in range(n)])  42.1 us
    unnamed x95, local copies, waits for them, and re-layouts  41.9 us
    ppermute x12, waiting for transfers between devices, swap(): return lax.ppermute(x, axis, [(i, i ^ d) for i in range(n)])  30.3 us
    pallas_call x5, Pallas kernels, relay(): pl.pallas_call(functools.partial(relay_kernel, first), in_specs=specs, ou...  27.6 us
    ppermute x32, waiting for transfers between devices, shift(): return lax.ppermute(x, axis, [(i, (i + d) % n) for i in range(n)])  19.1 us
    ppermute x12, starting transfers between devices, swap(): return lax.ppermute(x, axis, [(i, i ^ d) for i in range(n)])  18.6 us
    pallas_call x1, Pallas kernels, forward(): pl.pallas_call(forward_kernel, grid=(micro,), in_specs=[SMEM, block, pl.B...  12.9 us
  transfers between devices with their start and end apart: 48, of which 21 were waited for; matrix products, arithmetic and copies ran while one was open for 7% of the time, Pallas kernels for 10%

profile of v1, /device:TPU:0, one launch (start us, length us, event | category | flops | bytes accessed | tf_op | source)
XLA Modules:
  0.0 308.3 jit_solution(7136004300956379497)
XLA Ops:
  1.5 3.2 %collective-permute-start.17 = (bf16[6,1536]{1,0:T(8,128)(2,1)S(1)}, bf16[6,1536]{1,0:T(8,128)(2,1)S(1)}, u32[]{:S(2)}, u32[]{:S(2)}) collective-permute-start(bf16[6,1536]{1,0:T(8,128)(2,1)S(1)} %dynamic_update_slice.5), channel_id=1, source_target_pairs={{0,16},{16,0},{1,17},{17,1},{2,18},{18,2},{3,19},{19,3},{4,20},{20... | collective-permute-start | bytes 55304 | tf_op jit(solution)/shard_map/ppermute | solution.py:455
  11.9 3.9 %collective-permute-start.19 = (bf16[6,1536]{1,0:T(8,128)(2,1)S(1)}, bf16[6,1536]{1,0:T(8,128)(2,1)S(1)}, u32[]{:S(2)}, u32[]{:S(2)}) collective-permute-start(bf16[6,1536]{1,0:T(8,128)(2,1)S(1)} %add.150), channel_id=1, source_target_pairs={{0,8},{4,12},{8,0},{12,4},{1,9},{5,13},{9,1},{13,5},{2,10},{6,14},... | collective-permute-start | bytes 55304 | tf_op jit(solution)/shard_map/ppermute | solution.py:455
  15.9 3.2 %collective-permute-start.2 = (bf16[2,48,768]{2,1,0:T(8,128)(2,1)S(1)}, bf16[2,48,768]{2,1,0:T(8,128)(2,1)S(1)}, u32[]{:S(2)}, u32[]{:S(2)}) collective-permute-start(bf16[2,48,768]{2,1,0:T(8,128)(2,1)S(1)} %pad_maximum_fusion), channel_id=1, source_target_pairs={{0,3},{1,0},{2,1},{3,2},{4,7},{5,4},{6,5},{7,6},{8,11},{9,8},{10,9... | collective-permute-start | bytes 442376 | tf_op jit(solution)/shard_map/ppermute | solution.py:450
  21.9 3.6 %collective-permute-start.4 = (bf16[1,48,768]{2,1,0:T(8,128)(2,1)S(1)}, bf16[1,48,768]{2,1,0:T(8,128)(2,1)S(1)}, u32[]{:S(2)}, u32[]{:S(2)}) collective-permute-start(bf16[1,48,768]{2,1,0:T(8,128)(2,1)S(1)} %slice.216), channel_id=1, source_target_pairs={{0,3},{1,0},{2,1},{3,2},{4,7},{5,4},{6,5},{7,6},{8,11},{9,8},{10,9... | collective-permute-start | bytes 221192 | tf_op jit(solution)/shard_map/ppermute | solution.py:450
  35.9 3.2 %collective-permute-start.14 = (bf16[8,48,768]{2,1,0:T(8,128)(2,1)}, bf16[8,48,768]{2,1,0:T(8,128)(2,1)S(1)}, u32[]{:S(2)}, u32[]{:S(2)}) collective-permute-start(bf16[8,48,768]{2,1,0:T(8,128)(2,1)} %constant_dynamic-update-slice_fusion.6.rest_5_), channel_id=1, source_target_pairs={{0,3},{1,0},{2,1},{3,2},{4,7},{5,4},{6,5},{7,6},{8,11},{9,8},{10,9... | collective-permute-start | bytes 1769480 | tf_op jit(solution)/shard_map/ppermute | solution.py:450
  46.4 3.1 %collective-permute-done.20 = bf16[6,1536]{1,0:T(8,128)(2,1)S(1)} collective-permute-done((bf16[6,1536]{1,0:T(8,128)(2,1)S(1)}, bf16[6,1536]{1,0:T(8,128)(2,1)S(1)}, u32[]{:S(2)}, u32[]{:S(2)}) %collective-permute-start.20) | collective-permute-done | bytes 18464 | tf_op jit(solution)/shard_map/ppermute | solution.py:455
  55.0 3.3 %collective-permute-start.8 = (bf16[4,48,768]{2,1,0:T(8,128)(2,1)S(1)}, bf16[4,48,768]{2,1,0:T(8,128)(2,1)S(1)}, u32[]{:S(2)}, u32[]{:S(2)}) collective-permute-start(bf16[4,48,768]{2,1,0:T(8,128)(2,1)S(1)} %slice.218), channel_id=1, source_target_pairs={{0,12},{4,0},{8,4},{12,8},{1,13},{5,1},{9,5},{13,9},{2,14},{6,2},{... | collective-permute-start | bytes 884744 | tf_op jit(solution)/shard_map/ppermute | solution.py:450
  58.4 3.6 %collective-permute-start.16 = (bf16[4,48,768]{2,1,0:T(8,128)(2,1)S(1)}, bf16[4,48,768]{2,1,0:T(8,128)(2,1)S(1)}, u32[]{:S(2)}, u32[]{:S(2)}) collective-permute-start(bf16[4,48,768]{2,1,0:T(8,128)(2,1)S(1)} %slice.224), channel_id=1, source_target_pairs={{0,3},{1,0},{2,1},{3,2},{4,7},{5,4},{6,5},{7,6},{8,11},{9,8},{10,9... | collective-permute-start | bytes 884744 | tf_op jit(solution)/shard_map/ppermute | solution.py:450
  65.0 12.9 %shard_map.156 = (bf16[2,512,1536]{2,1,0:T(8,128)(2,1)S(1)}, bf16[2,512,1536]{2,1,0:T(8,128)(2,1)S(1)}, f32[2,512,128]{2,1,0:T(8,128)S(1)}, bf16[2,512,1536]{2,1,0:T(8,128)(2,1)S(1)}) custom-call(s32[2]{0:T(128)S(1)} %bitcast.55, bf16[2,512,1536]{2,1,0:T(8,128)(2,1)S(1)} %bitcast.57, f32[8,1536]{1,0:T(8,128)S(1)} %pad_convert_fusion.taps.rest_13_), custom_call_target="tpu_custom_call" | custom-call | flops 12000000000 | bytes 1048576 | tf_op jit(solution)/shard_map/pallas_call | solution.py:114
  100.9 2.9 collective-permute-done.23.come
  111.6 47.5 %collective-permute-done.24.come = bf16[512,1536]{1,0:T(8,128)(2,1)} collective-permute-done((bf16[512,1536]{1,0:T(8,128)(2,1)}, bf16[512,1536]{1,0:T(8,128)(2,1)}, u32[]{:S(2)}, u32[]{:S(2)}) %collective-permute-start.24) | collective-permute-done | bytes 1572896 | tf_op jit(solution)/shard_map/ppermute | solution.py:532
  162.1 12.6 %shard_map.160 = (bf16[512,1536]{1,0:T(8,128)(2,1)}, bf16[2,512,1536]{2,1,0:T(8,128)(2,1)}, bf16[2,512,1536]{2,1,0:T(8,128)(2,1)S(1)}, f32[2,12,528,128]{3,2,1,0:T(8,128)}, f32[2,8,1536]{2,1,0:T(8,128)S(1)}) custom-call(s32[88]{0:T(128)S(1)} %concatenate.37.step, ...), custom_call_target="tpu_custom_call", output_to_operand_aliasing={{1}: (17, {}), {2}: (18, {}), {3}: (19, {}), {4}: (20, {})} | custom-call | flops 8000000000 | bytes 1048576 | tf_op jit(solution)/shard_map/pallas_call | solution.py:276
  180.3 17.5 %collective-permute-done.25.come = bf16[512,1536]{1,0:T(8,128)(2,1)} collective-permute-done((bf16[512,1536]{1,0:T(8,128)(2,1)}, bf16[512,1536]{1,0:T(8,128)(2,1)}, u32[]{:S(2)}, u32[]{:S(2)}) %collective-permute-start.25) | collective-permute-done | bytes 1572896 | tf_op jit(solution)/shard_map/ppermute | solution.py:532
  201.5 12.1 %shard_map.162 = (bf16[8,48,768]{2,1,0:T(8,128)(2,1)S(1)}, bf16[8,48,768]{2,1,0:T(8,128)(2,1)S(1)}, bf16[16,48,768]{2,1,0:T(8,128)(2,1)S(1)}, bf16[8,48,768]{2,1...) custom-call(s32[72]{0:T(128)S(1)} %concatenate.44.step, ...), custom_call_target="tpu_custom_call" | custom-call | flops 8000000000 | bytes 1048576 | tf_op jit(solution)/shard_map/pallas_call | solution.py:370
  213.6 3.0 collective-permute-start.26
  216.6 3.0 collective-permute-start.33
  221.5 12.8 %shard_map.161 = (bf16[512,1536]{1,0:T(8,128)(2,1)}, bf16[2,512,1536]{2,1,0:T(8,128)(2,1)}, bf16[2,512,1536]{2,1,0:T(8,128)(2,1)S(1)}, f32[2,12,528,128]{3,2,1,0:T(8,128)}, f32[2,8,1536]{2,1,0:T(8,128)S(1)}) custom-call(s32[88]{0:T(128)S(1)} %concatenate.36.step, ...), custom_call_target="tpu_custom_call", output_to_operand_aliasing={{1}: (17, {}), {2}: (18, {}), {3}: (19, {}), {4}: (20, {})} | custom-call | flops 8000000000 | bytes 1048576 | tf_op jit(solution)/shard_map/pallas_call | solution.py:276
  237.2 5.5 %shard_map.163 = f32[8,1536]{1,0:T(8,128)S(1)} custom-call(s32[2]{0:T(128)S(1)} %bitcast.56, bf16[2,512,1536]{2,1,0:T(8,128)(2,1)S(1)} %bitcast.58, f32[2,12,528,128]{3,2,1,0:T(8,128)S(1)} %copy-done.18, f32[2,8,1536]{2,1,0:T(8,128)S(1)} %get-tuple-element.69.gain_ref, f32[8,1536]{1,0:T(8,128)S(1)} %pad_convert_fusion.taps.rest_13_), custom_call_target="tpu_custom_call" | custom-call | flops 8000000000 | bytes 1048576 | tf_op jit(solution)/shard_map/pallas_call | solution.py:430
  248.4 4.1 %collective-permute-done.44 = f32[8,1536]{1,0:T(8,128)S(1)} collective-permute-done((f32[8,1536]{1,0:T(8,128)S(1)}, f32[8,1536]{1,0:T(8,128)S(1)}, u32[]{:S(2)}, u32[]{:S(2)}) %collective-permute-start.44) | collective-permute-done | bytes 49184 | tf_op jit(solution)/shard_map/ppermute | solution.py:455
  252.7 5.9 %collective-permute-done.45 = f32[8,1536]{1,0:T(8,128)S(1)} collective-permute-done((f32[8,1536]{1,0:T(8,128)S(1)}, f32[8,1536]{1,0:T(8,128)S(1)}, u32[]{:S(2)}, u32[]{:S(2)}) %collective-permute-start.45) | collective-permute-done | bytes 49184 | tf_op jit(solution)/shard_map/ppermute | solution.py:455
  264.2 9.8 %collective-permute-done.47 = f32[8,1536]{1,0:T(8,128)S(1)} collective-permute-done((f32[8,1536]{1,0:T(8,128)S(1)}, f32[8,1536]{1,0:T(8,128)S(1)}, u32[]{:S(2)}, u32[]{:S(2)}) %collective-permute-start.47) | collective-permute-done | bytes 49184 | tf_op jit(solution)/shard_map/ppermute | solution.py:455
  275.7 5.3 %collective-permute-done.34 = bf16[4,48,768]{2,1,0:T(8,128)(2,1)S(1)} collective-permute-done((bf16[4,48,768]{2,1,0:T(8,128)(2,1)S(1)}, bf16[4,48,768]{2,1,0:T(8,128)(2,1)S(1)}, u32[]{:S(2)}, u32[]{:S(2)}) %collective-permute-start.34) | collective-permute-done | bytes 294944 | tf_op jit(solution)/shard_map/ppermute | solution.py:450
  285.6 3.8 %collective-permute-done.36 = bf16[4,48,768]{2,1,0:T(8,128)(2,1)S(1)} collective-permute-done((bf16[4,48,768]{2,1,0:T(8,128)(2,1)S(1)}, bf16[4,48,768]{2,1,0:T(8,128)(2,1)S(1)}, u32[]{:S(2)}, u32[]{:S(2)}) %collective-permute-start.36) | collective-permute-done | bytes 294944 | tf_op jit(solution)/shard_map/ppermute | solution.py:450
  295.0 3.7 %collective-permute-start.41 = (bf16[1,48,768]{2,1,0:T(8,128)(2,1)S(1)}, bf16[1,48,768]{2,1,0:T(8,128)(2,1)S(1)}, u32[]{:S(2)}, u32[]{:S(2)}) collective-permute-start(bf16[1,48,768]{2,1,0:T(8,128)(2,1)S(1)} %add_convert_fusion.9), channel_id=1, source_target_pairs={{0,12},{4,0},{8,4},{12,8},{1,13},{5,1},{9,5},{13,9},{2,14},{6,2},{... | collective-permute-start | bytes 221192 | tf_op jit(solution)/shard_map/ppermute | solution.py:450
  (239 shorter events, 110.9 us)
Async XLA Ops:
  4.7 11.1 %collective-permute-start = (bf16[48,1536]{1,0:T(8,128)(2,1)}, bf16[48,1536]{1,0:T(8,128)(2,1)S(1)}, u32[]{:S(2)}, u32[]{:S(2)}) collective-permute-start(bf16[48,1536]{1,0:T(8,128)(2,1)} %bitcast.64), channel_id=1, source_target_pairs={{0,16},{16,0},{1,17},{17,1},{2,18},{18,2},{3,19},{19,3},{4,20},{20... | collective-permute-start | bytes 442376 | tf_op jit(solution)/shard_map/ppermute | solution.py:455
  11.9 33.7 %collective-permute-start.19 = (bf16[6,1536]{1,0:T(8,128)(2,1)S(1)}, bf16[6,1536]{1,0:T(8,128)(2,1)S(1)}, u32[]{:S(2)}, u32[]{:S(2)}) collective-permute-start(bf16[6,1536]{1,0:T(8,128)(2,1)S(1)} %add.150), channel_id=1, source_target_pairs={{0,8},{4,12},{8,0},{12,4},{1,9},{5,13},{9,1},{13,5},{2,10},{6,14},... | collective-permute-start | bytes 55304 | tf_op jit(solution)/shard_map/ppermute | solution.py:455
  21.9 9.8 %collective-permute-start.4 = (bf16[1,48,768]{2,1,0:T(8,128)(2,1)S(1)}, bf16[1,48,768]{2,1,0:T(8,128)(2,1)S(1)}, u32[]{:S(2)}, u32[]{:S(2)}) collective-permute-start(bf16[1,48,768]{2,1,0:T(8,128)(2,1)S(1)} %slice.216), channel_id=1, source_target_pairs={{0,3},{1,0},{2,1},{3,2},{4,7},{5,4},{6,5},{7,6},{8,11},{9,8},{10,9... | collective-permute-start | bytes 221192 | tf_op jit(solution)/shard_map/ppermute | solution.py:450
  25.6 9.6 %collective-permute-start.12 = (bf16[1,48,768]{2,1,0:T(8,128)(2,1)S(1)}, bf16[1,48,768]{2,1,0:T(8,128)(2,1)S(1)}, u32[]{:S(2)}, u32[]{:S(2)}) collective-permute-start(bf16[1,48,768]{2,1,0:T(8,128)(2,1)S(1)} %slice.222), channel_id=1, source_target_pairs={{0,12},{4,0},{8,4},{12,8},{1,13},{5,1},{9,5},{13,9},{2,14},{6,2},{... | collective-permute-start | bytes 221192 | tf_op jit(solution)/shard_map/ppermute | solution.py:450
  32.4 22.5 %collective-permute-start.6 = (bf16[8,48,768]{2,1,0:T(8,128)(2,1)}, bf16[8,48,768]{2,1,0:T(8,128)(2,1)S(1)}, u32[]{:S(2)}, u32[]{:S(2)}) collective-permute-start(bf16[8,48,768]{2,1,0:T(8,128)(2,1)} %constant_dynamic-update-slice_fusion.rest_0_), channel_id=1, source_target_pairs={{0,12},{4,0},{8,4},{12,8},{1,13},{5,1},{9,5},{13,9},{2,14},{6,2},{... | collective-permute-start | bytes 1769480 | tf_op jit(solution)/shard_map/ppermute | solution.py:450
  34.6 23.7 %collective-permute-start.5 = (bf16[8,48,768]{2,1,0:T(8,128)(2,1)}, bf16[8,48,768]{2,1,0:T(8,128)(2,1)S(1)}, u32[]{:S(2)}, u32[]{:S(2)}) collective-permute-start(bf16[8,48,768]{2,1,0:T(8,128)(2,1)} %constant_dynamic-update-slice_fusion.rest_0_), channel_id=1, source_target_pairs={{0,4},{4,8},{8,12},{12,0},{1,5},{5,9},{9,13},{13,1},{2,6},{6,10},{... | collective-permute-start | bytes 1769480 | tf_op jit(solution)/shard_map/ppermute | solution.py:450
  35.9 22.5 %collective-permute-start.14 = (bf16[8,48,768]{2,1,0:T(8,128)(2,1)}, bf16[8,48,768]{2,1,0:T(8,128)(2,1)S(1)}, u32[]{:S(2)}, u32[]{:S(2)}) collective-permute-start(bf16[8,48,768]{2,1,0:T(8,128)(2,1)} %constant_dynamic-update-slice_fusion.6.rest_5_), channel_id=1, source_target_pairs={{0,3},{1,0},{2,1},{3,2},{4,7},{5,4},{6,5},{7,6},{8,11},{9,8},{10,9... | collective-permute-start | bytes 1769480 | tf_op jit(solution)/shard_map/ppermute | solution.py:450
  39.1 22.9 %collective-permute-start.13 = (bf16[8,48,768]{2,1,0:T(8,128)(2,1)}, bf16[8,48,768]{2,1,0:T(8,128)(2,1)}, u32[]{:S(2)}, u32[]{:S(2)}) collective-permute-start(bf16[8,48,768]{2,1,0:T(8,128)(2,1)} %constant_dynamic-update-slice_fusion.6.rest_5_), channel_id=1, source_target_pairs={{0,1},{1,2},{2,3},{3,0},{4,5},{5,6},{6,7},{7,4},{8,9},{9,10},{10,1... | collective-permute-start | bytes 1769480 | tf_op jit(solution)/shard_map/ppermute | solution.py:450
  55.0 28.0 %collective-permute-start.8 = (bf16[4,48,768]{2,1,0:T(8,128)(2,1)S(1)}, bf16[4,48,768]{2,1,0:T(8,128)(2,1)S(1)}, u32[]{:S(2)}, u32[]{:S(2)}) collective-permute-start(bf16[4,48,768]{2,1,0:T(8,128)(2,1)S(1)} %slice.218), channel_id=1, source_target_pairs={{0,12},{4,0},{8,4},{12,8},{1,13},{5,1},{9,5},{13,9},{2,14},{6,2},{... | collective-permute-start | bytes 884744 | tf_op jit(solution)/shard_map/ppermute | solution.py:450
  58.3 24.7 %collective-permute-start.7 = (bf16[4,48,768]{2,1,0:T(8,128)(2,1)S(1)}, bf16[4,48,768]{2,1,0:T(8,128)(2,1)S(1)}, u32[]{:S(2)}, u32[]{:S(2)}) collective-permute-start(bf16[4,48,768]{2,1,0:T(8,128)(2,1)S(1)} %slice.217), channel_id=1, source_target_pairs={{0,4},{4,8},{8,12},{12,0},{1,5},{5,9},{9,13},{13,1},{2,6},{6,10},{... | collective-permute-start | bytes 884744 | tf_op jit(solution)/shard_map/ppermute | solution.py:450
  58.4 24.6 %collective-permute-start.16 = (bf16[4,48,768]{2,1,0:T(8,128)(2,1)S(1)}, bf16[4,48,768]{2,1,0:T(8,128)(2,1)S(1)}, u32[]{:S(2)}, u32[]{:S(2)}) collective-permute-start(bf16[4,48,768]{2,1,0:T(8,128)(2,1)S(1)} %slice.224), channel_id=1, source_target_pairs={{0,3},{1,0},{2,1},{3,2},{4,7},{5,4},{6,5},{7,6},{8,11},{9,8},{10,9... | collective-permute-start | bytes 884744 | tf_op jit(solution)/shard_map/ppermute | solution.py:450
  63.0 20.0 %collective-permute-start.15 = (bf16[4,48,768]{2,1,0:T(8,128)(2,1)S(1)}, bf16[4,48,768]{2,1,0:T(8,128)(2,1)S(1)}, u32[]{:S(2)}, u32[]{:S(2)}) collective-permute-start(bf16[4,48,768]{2,1,0:T(8,128)(2,1)S(1)} %slice.223), channel_id=1, source_target_pairs={{0,1},{1,2},{2,3},{3,0},{4,5},{5,6},{6,7},{7,4},{8,9},{9,10},{10,1... | collective-permute-start | bytes 884744 | tf_op jit(solution)/shard_map/ppermute | solution.py:450
  109.0 50.1 %collective-permute-start.24 = (bf16[512,1536]{1,0:T(8,128)(2,1)}, bf16[512,1536]{1,0:T(8,128)(2,1)}, u32[]{:S(2)}, u32[]{:S(2)}) collective-permute-start(bf16[512,1536]{1,0:T(8,128)(2,1)} %get-tuple-element.50), channel_id=1, source_target_pairs={{96,64},{64,32},{32,0},{97,65},{65,33},{33,1},{98,66},{66,34},{34,... | collective-permute-start | bytes 4718600 | tf_op jit(solution)/shard_map/ppermute | solution.py:532
  176.3 21.4 %collective-permute-start.25 = (bf16[512,1536]{1,0:T(8,128)(2,1)}, bf16[512,1536]{1,0:T(8,128)(2,1)}, u32[]{:S(2)}, u32[]{:S(2)}) collective-permute-start(bf16[512,1536]{1,0:T(8,128)(2,1)} %get-tuple-element.55), channel_id=1, source_target_pairs={{32,0},{33,1},{34,2},{35,3},{36,4},{37,5},{38,6},{39,7},{40,8},{41... | collective-permute-start | bytes 4718600 | tf_op jit(solution)/shard_map/ppermute | solution.py:532
  213.6 49.3 %collective-permute-start.26 = (bf16[8,48,768]{2,1,0:T(8,128)(2,1)S(1)}, bf16[8,48,768]{2,1,0:T(8,128)(2,1)S(1)}, u32[]{:S(2)}, u32[]{:S(2)}) collective-permute-start(bf16[8,48,768]{2,1,0:T(8,128)(2,1)S(1)} %get-tuple-element.63), channel_id=1, source_target_pairs={{0,12},{4,0},{8,4},{12,8},{1,13},{5,1},{9,5},{13,9},{2,14},{6,2},{... | collective-permute-start | bytes 1769480 | tf_op jit(solution)/shard_map/ppermute | solution.py:450
  216.6 57.5 %collective-permute-start.33 = (bf16[8,48,768]{2,1,0:T(8,128)(2,1)S(1)}, bf16[8,48,768]{2,1,0:T(8,128)(2,1)S(1)}, u32[]{:S(2)}, u32[]{:S(2)}) collective-permute-start(bf16[8,48,768]{2,1,0:T(8,128)(2,1)S(1)} %get-tuple-element.66), channel_id=1, source_target_pairs={{0,3},{1,0},{2,1},{3,2},{4,7},{5,4},{6,5},{7,6},{8,11},{9,8},{10,9... | collective-permute-start | bytes 1769480 | tf_op jit(solution)/shard_map/ppermute | solution.py:450
  258.7 15.6 %collective-permute-start.28 = (bf16[8,48,768]{2,1,0:T(8,128)(2,1)S(1)}, bf16[8,48,768]{2,1,0:T(8,128)(2,1)S(1)}, u32[]{:S(2)}, u32[]{:S(2)}) collective-permute-start(bf16[8,48,768]{2,1,0:T(8,128)(2,1)S(1)} %get-tuple-element.64), channel_id=1, source_target_pairs={{0,4},{4,8},{8,12},{12,0},{1,5},{5,9},{9,13},{13,1},{2,6},{6,10},{... | collective-permute-start | bytes 1769480 | tf_op jit(solution)/shard_map/ppermute | solution.py:450
  258.8 16.9 %collective-permute-start.35 = (bf16[8,48,768]{2,1,0:T(8,128)(2,1)S(1)}, bf16[8,48,768]{2,1,0:T(8,128)(2,1)S(1)}, u32[]{:S(2)}, u32[]{:S(2)}) collective-permute-start(bf16[8,48,768]{2,1,0:T(8,128)(2,1)S(1)} %get-tuple-element.67), channel_id=1, source_target_pairs={{0,1},{1,2},{2,3},{3,0},{4,5},{5,6},{6,7},{7,4},{8,9},{9,10},{10,1... | collective-permute-start | bytes 1769480 | tf_op jit(solution)/shard_map/ppermute | solution.py:450
  262.8 11.2 %collective-permute-start.47 = (f32[8,1536]{1,0:T(8,128)S(1)}, f32[8,1536]{1,0:T(8,128)S(1)}, u32[]{:S(2)}, u32[]{:S(2)}) collective-permute-start(f32[8,1536]{1,0:T(8,128)S(1)} %add.182), channel_id=1, source_target_pairs={{0,2},{1,3},{2,0},{3,1},{4,6},{5,7},{6,4},{7,5},{8,10},{9,11},{10,... | collective-permute-start | bytes 147464 | tf_op jit(solution)/shard_map/ppermute | solution.py:455
  263.0 11.3 %collective-permute-start.27 = (bf16[4,48,768]{2,1,0:T(8,128)(2,1)S(1)}, bf16[4,48,768]{2,1,0:T(8,128)(2,1)S(1)}, u32[]{:S(2)}, u32[]{:S(2)}) collective-permute-start(bf16[4,48,768]{2,1,0:T(8,128)(2,1)S(1)} %add_convert_fusion.7), channel_id=1, source_target_pairs={{0,12},{4,0},{8,4},{12,8},{1,13},{5,1},{9,5},{13,9},{2,14},{6,2},{... | collective-permute-start | bytes 884744 | tf_op jit(solution)/shard_map/ppermute | solution.py:450
  274.5 8.8 %collective-permute-start.29 = (bf16[4,48,768]{2,1,0:T(8,128)(2,1)S(1)}, bf16[4,48,768]{2,1,0:T(8,128)(2,1)S(1)}, u32[]{:S(2)}, u32[]{:S(2)}) collective-permute-start(bf16[4,48,768]{2,1,0:T(8,128)(2,1)S(1)} %get-tuple-element.75), channel_id=1, source_target_pairs={{0,4},{4,8},{8,12},{12,0},{1,5},{5,9},{9,13},{13,1},{2,6},{6,10},{... | collective-permute-start | bytes 884744 | tf_op jit(solution)/shard_map/ppermute | solution.py:450
  281.2 8.2 %collective-permute-start.36 = (bf16[4,48,768]{2,1,0:T(8,128)(2,1)S(1)}, bf16[4,48,768]{2,1,0:T(8,128)(2,1)S(1)}, u32[]{:S(2)}, u32[]{:S(2)}) collective-permute-start(bf16[4,48,768]{2,1,0:T(8,128)(2,1)S(1)} %get-tuple-element.77), channel_id=1, source_target_pairs={{0,1},{1,2},{2,3},{3,0},{4,5},{5,6},{6,7},{7,4},{8,9},{9,10},{10,1... | collective-permute-start | bytes 884744 | tf_op jit(solution)/shard_map/ppermute | solution.py:450
  283.4 8.9 %collective-permute-start.32 = (bf16[2,48,768]{2,1,0:T(8,128)(2,1)S(1)}, bf16[2,48,768]{2,1,0:T(8,128)(2,1)S(1)}, u32[]{:S(2)}, u32[]{:S(2)}) collective-permute-start(bf16[2,48,768]{2,1,0:T(8,128)(2,1)S(1)} %get-tuple-element.82), channel_id=1, source_target_pairs={{0,3},{1,0},{2,1},{3,2},{4,7},{5,4},{6,5},{7,6},{8,11},{9,8},{10,9... | collective-permute-start | bytes 442376 | tf_op jit(solution)/shard_map/ppermute | solution.py:450
  285.3 13.4 %collective-permute-start.30 = (bf16[2,48,768]{2,1,0:T(8,128)(2,1)S(1)}, bf16[2,48,768]{2,1,0:T(8,128)(2,1)S(1)}, u32[]{:S(2)}, u32[]{:S(2)}) collective-permute-start(bf16[2,48,768]{2,1,0:T(8,128)(2,1)S(1)} %get-tuple-element.83), channel_id=1, source_target_pairs={{0,1},{1,2},{2,3},{3,0},{4,5},{5,6},{6,7},{7,4},{8,9},{9,10},{10,1... | collective-permute-start | bytes 442376 | tf_op jit(solution)/shard_map/ppermute | solution.py:450
  (67 other events, 483.5 us)

commit v2 on v1

v2 whole, which is shorter than its diff:
```python
import functools

import jax
import jax.numpy as jnp
import numpy as np
from jax import lax
from jax.experimental import pallas as pl
from jax.experimental.pallas import tpu as pltpu
from jax.sharding import Mesh
from jax.sharding import PartitionSpec as P

EPSILON = 1e-05
F32 = jnp.float32
BF16 = jnp.bfloat16
LANES = 128
PAD = 8
ANY = pl.BlockSpec(memory_space=pl.ANY)
HBM = pl.BlockSpec(memory_space=pltpu.HBM)
SMEM = pl.BlockSpec(memory_space=pltpu.SMEM)
VMEM = pl.BlockSpec(memory_space=pltpu.VMEM)

GATHERED = [(0, 0), (0, 1), (3, 0), (3, 1), (1, 0), (1, 1), (2, 0), (2, 1)]
SCATTERED = [(2, 0), (1, 1), (2, 1), (3, 0), (1, 0), (3, 1), (0, 0), (0, 1)]


def params(limit, **kw):
    return pltpu.CompilerParams(vmem_limit_bytes=limit << 20, **kw)


def cost(us):
    return pl.CostEstimate(flops=int(us * 1.0e9), bytes_accessed=1 << 20, transcendentals=0)


def tables():
    gather = np.zeros((2, 4, 4, 2, 5, 8), np.int32)
    scatter = np.zeros((2, 4, 4, 2, 32), np.int32)
    for x in range(2):
        for z in range(4):
            for y in range(4):
                for half in range(2):
                    inner, outer = (y, z) if half == 0 else (z, y)

                    def block(o, i, r):
                        a, b, c = (outer + o) % 4, (inner + i) % 4, (x + r) % 2
                        zz, yy = (a, b) if half == 0 else (b, a)
                        return c * 16 + zz * 4 + yy

                    for slot, o in enumerate((0, 3, 1, 2)):
                        for j, (i, r) in enumerate(GATHERED):
                            gather[x, z, y, half, slot, j] = block(o, i, r)
                    for o in range(4):
                        for j, (i, r) in enumerate(SCATTERED):
                            base = {2: (0, 8), 1: (16, 4), 3: (12, 20), 0: (24, 28)}[o]
                            place = base[0] + j if j < 4 else base[1] + j - 4
                            scatter[x, z, y, half, block(o, i, r)] = place
    return gather.reshape(2, 4, 4, -1), scatter.reshape(2, 4, 4, -1)


def forward_kernel(m, lens, x_in, taps, normed_ref, slope_ref, inv_ref, act_ref, x_ref, hid, mix, act, sem):
    length = lens[m]
    frames, feats = x_ref.shape
    cols = feats // LANES
    copy = pltpu.make_async_copy(x_in.at[m], x_ref, sem)
    copy.start()
    for c in range(cols):
        hid[c, 0:PAD, :] = jnp.zeros((PAD, LANES), F32)
        hid[c, PAD + frames : 2 * PAD + frames, :] = jnp.zeros((PAD, LANES), F32)
    copy.wait()

    def load(i, carry):
        r = pl.multiple_of(i * 16, 16)
        rows = r + lax.broadcasted_iota(jnp.int32, (16, LANES), 0)
        keep = rows < length
        for c in range(cols):
            v = x_ref[pl.ds(r, 16), c * LANES : (c + 1) * LANES].astype(F32)
            hid[c, pl.ds(r + PAD, 16), :] = jnp.where(keep, v, 0.0)
        return carry

    lax.fori_loop(0, frames // 16, load, 0, unroll=2)

    def conv(i, carry):
        r = pl.multiple_of(i * 64, 64)
        for c in range(cols):
            span = slice(c * LANES, (c + 1) * LANES)
            total = taps[0:1, span] * hid[c, pl.ds(r + PAD - 2, 64), :]
            for k in range(1, 5):
                total = total + taps[k : k + 1, span] * hid[c, pl.ds(r + PAD - 2 + k, 64), :]
            mix[pl.ds(r, 64), span] = total
        return carry

    lax.fori_loop(0, frames // 64, conv, 0)

    def norm(i, carry):
        r = pl.multiple_of(i * 16, 16)
        keep = r + lax.broadcasted_iota(jnp.int32, (16, 1), 0) < length
        mixed = mix[pl.ds(r, 16), :]
        centred = mixed - jnp.mean(mixed, axis=-1, keepdims=True)
        inverse = lax.rsqrt(jnp.mean(centred * centred, axis=-1, keepdims=True) + EPSILON)
        gain = taps[5:6, :]
        normed = centred * inverse
        gained = normed * gain
        logistic = jax.nn.sigmoid(gained)
        normed_ref[pl.ds(r, 16), :] = normed.astype(BF16)
        slope_ref[pl.ds(r, 16), :] = (
            (logistic + gained * logistic * (1.0 - logistic)) * gain
        ).astype(BF16)
        act[pl.ds(r, 16), :] = jnp.where(keep, gained * logistic, 0.0).astype(BF16)
        inv_ref[pl.ds(r, 16), :] = jnp.broadcast_to(inverse, (16, LANES))
        return carry

    lax.fori_loop(0, frames // 16, norm, 0, unroll=2)

    for c in range(feats // 256):
        act_ref[c * 256 : (c + 1) * 256, :] = act[:, c * 256 : (c + 1) * 256].T


def forward(m, lens, x, taps):
    micro, frames, feats = x.shape
    return pl.pallas_call(
        functools.partial(forward_kernel, m),
        in_specs=[SMEM, HBM, VMEM],
        out_specs=[VMEM] * 4,
        out_shape=[
            jax.ShapeDtypeStruct((frames, feats), BF16),
            jax.ShapeDtypeStruct((frames, feats), BF16),
            jax.ShapeDtypeStruct((frames, LANES), F32),
            jax.ShapeDtypeStruct((feats, frames), BF16),
        ],
        scratch_shapes=[
            pltpu.VMEM((frames, feats), BF16),
            pltpu.VMEM((feats // LANES, frames + 2 * PAD, LANES), F32),
            pltpu.VMEM((frames, feats), F32),
            pltpu.VMEM((frames, feats), BF16),
            pltpu.SemaphoreType.DMA,
        ],
        compiler_params=params(60),
        cost_estimate=cost(8),
    )(lens, x, taps)


def relay_kernel(first, who, meta, grads, come, come_one, *rest):
    (wa, wb), rest = (rest[:5], rest[5:10]), rest[10:]
    (normed_in, slope_in, inv_in), taps, rest = (rest[0:2], rest[2:4], rest[4:6]), rest[6], rest[7:]
    if not first:
        rest = rest[2:]
    send, mixed_out, gain_out = rest[:3]
    w, up, normed, slope, inv, ga, gmix, narrow, out, gsum, sems = rest[3:]
    frames, feats = up.shape
    cols = feats // LANES
    half = feats // 2
    rows = 48
    head = 288
    section = meta[0]
    turn = sum(jnp.where(section == i, m, 0) for i, m in enumerate(who))
    active, slot = turn >= 0, jnp.maximum(turn, 0)
    last, length = section == 3, meta[1 + slot]

    def pieces():
        made = []
        for h, parts in enumerate((wa, wb)):
            for p in range(5):
                for j in range(parts[p].shape[0]):
                    at = h * 40 + (p * 8 + j if p < 4 else 28 + j)
                    place = pl.multiple_of(meta[8 + at] * rows, 16)
                    made.append(
                        pltpu.make_async_copy(
                            parts[p].at[j],
                            w.at[pl.ds(place, rows), pl.ds(h * half, half)],
                            sems.at[0],
                        )
                    )
        return made

    def fetch(source):
        pltpu.make_async_copy(source.at[pl.ds(0, head)], up.at[pl.ds(0, head)], sems.at[1]).start()
        pltpu.make_async_copy(
            source.at[pl.ds(head, frames - head)], up.at[pl.ds(head, frames - head)], sems.at[8]
        ).start()

    @pl.when(active)
    def _():
        @pl.when(last)
        def _():
            fetch(grads.at[slot])

        @pl.when(section == 1)
        def _():
            fetch(come_one)

        @pl.when(jnp.logical_and(section != 3, section != 1))
        def _():
            fetch(come)

        weights = pieces()
        for copy in weights:
            copy.start()
        for m in range(2):

            @pl.when(slot == m)
            def _():
                pltpu.make_async_copy(normed_in[m], normed, sems.at[2]).start()
                pltpu.make_async_copy(slope_in[m], slope, sems.at[3]).start()
                pltpu.make_async_copy(inv_in[m], inv, sems.at[4]).start()

        for c in range(cols):
            gmix[c, 0:PAD, :] = jnp.zeros((PAD, LANES), F32)
            gmix[c, PAD + frames : 2 * PAD + frames, :] = jnp.zeros((PAD, LANES), F32)
        gsum[...] = jnp.zeros_like(gsum)

        def multiply(start, size, n):
            r = pl.multiple_of(n * 256, 256)
            ga[start : start + size, pl.ds(r, 256)] = lax.dot_general(
                up[start : start + size, :],
                w[pl.ds(r, 256), :],
                (((1,), (1,)), ((), ())),
                preferred_element_type=F32,
            )

        def through(i):
            r = pl.multiple_of(i * 16, 16)
            keep = r + lax.broadcasted_iota(jnp.int32, (16, 1), 0) < length
            gn = ga[pl.ds(r, 16), :] * slope[pl.ds(r, 16), :].astype(F32)
            gn = jnp.where(keep, gn, 0.0)
            nm = normed[pl.ds(r, 16), :].astype(F32)
            both = gn * nm
            gsum[...] += both[:8] + both[8:]
            a = jnp.sum(gn, axis=-1, keepdims=True) * (1.0 / feats)
            b = jnp.sum(both, axis=-1, keepdims=True) * (1.0 / feats)
            mixed = inv[pl.ds(r, 16), 0:1] * (gn - a - nm * b)
            narrow[pl.ds(r, 16), :] = mixed.astype(BF16)
            for c in range(cols):
                gmix[c, pl.ds(r + PAD, 16), :] = mixed[:, c * LANES : (c + 1) * LANES]

        def first_part(n, carry):
            multiply(0, head, n)
            return carry

        def second_part(n, carry):
            multiply(head, frames - head, n)
            for q in range(3):
                through(n * 3 + q)
            return carry

        def third_part(n, carry):
            for q in range(2):
                through(head // 16 + n * 2 + q)
            return carry

        pltpu.make_async_copy(come.at[pl.ds(0, head)], up.at[pl.ds(0, head)], sems.at[1]).wait()
        for copy in weights:
            copy.wait()
        lax.fori_loop(0, feats // 256, first_part, 0)
        pltpu.make_async_copy(
            come.at[pl.ds(head, frames - head)], up.at[pl.ds(head, frames - head)], sems.at[8]
        ).wait()
        pltpu.make_async_copy(normed_in[0], normed, sems.at[2]).wait()
        pltpu.make_async_copy(slope_in[0], slope, sems.at[3]).wait()
        pltpu.make_async_copy(inv_in[0], inv, sems.at[4]).wait()
        lax.fori_loop(0, feats // 256, second_part, 0)
        upper, lower = pl.ds(0, head), pl.ds(head, frames - head)
        early = pltpu.make_async_copy(narrow.at[upper], mixed_out.at[slot, upper], sems.at[9])
        early.start()
        lax.fori_loop(0, (frames - head) // 32, third_part, 0)
        saved = [
            pltpu.make_async_copy(narrow.at[lower], mixed_out.at[slot, lower], sems.at[5]),
            pltpu.make_async_copy(gsum, gain_out.at[slot], sems.at[6]),
        ]
        for copy in saved:
            copy.start()

        def conv(i, carry):
            r = pl.multiple_of(i * 64, 64)
            keep = r + lax.broadcasted_iota(jnp.int32, (64, LANES), 0) < length
            for c in range(cols):
                span = slice(c * LANES, (c + 1) * LANES)
                total = taps[4:5, span] * gmix[c, pl.ds(r + PAD - 2, 64), :]
                for k in range(1, 5):
                    total = total + taps[4 - k : 5 - k, span] * gmix[c, pl.ds(r + PAD - 2 + k, 64), :]
                result = up[pl.ds(r, 64), span].astype(F32) + jnp.where(keep, total, 0.0)
                out[pl.ds(r, 64), span] = result.astype(BF16)
            part = pl.ds(r, 64)
            pltpu.make_async_copy(out.at[part], send.at[part], sems.at[7]).start()
            return carry

        lax.fori_loop(0, frames // 64, conv, 0)
        pltpu.make_async_copy(out, send, sems.at[7]).wait()
        for copy in [early] + saved:
            copy.wait()


def relay(who, meta, grads, come, come_one, weights, saved, taps, state):
    micro, frames, feats = grads.shape
    cols = feats // LANES
    first = state is None
    shapes = [
        jax.ShapeDtypeStruct((frames, feats), BF16),
        jax.ShapeDtypeStruct((micro, frames, feats), BF16),
        jax.ShapeDtypeStruct((micro, 8, feats), F32),
    ]
    operands = [meta, grads, come, come_one, *weights, *saved, taps]
    specs = [SMEM, HBM, ANY, ANY] + [HBM] * (len(operands) - 5) + [VMEM]
    aliases = {}
    if not first:
        aliases = {len(operands) + i: 1 + i for i in range(2)}
        operands += list(state)
        specs += [HBM] * 2
    out = pl.pallas_call(
        functools.partial(relay_kernel, first, who),
        in_specs=specs,
        out_specs=[ANY] + [HBM] * 2,
        out_shape=shapes,
        input_output_aliases=aliases,
        scratch_shapes=[
            pltpu.VMEM((feats, feats), BF16),
            pltpu.VMEM((frames, feats), BF16),
            pltpu.VMEM((frames, feats), BF16),
            pltpu.VMEM((frames, feats), BF16),
            pltpu.VMEM((frames, LANES), F32),
            pltpu.VMEM((frames, feats), F32),
            pltpu.VMEM((cols, frames + 2 * PAD, LANES), F32),
            pltpu.VMEM((frames, feats), BF16),
            pltpu.VMEM((frames, feats), BF16),
            pltpu.VMEM((8, feats), F32),
            pltpu.SemaphoreType.DMA((10,)),
        ],
        compiler_params=params(60),
        cost_estimate=cost(1),
    )(*operands)
    return out[0], tuple(out[1:])


def weight_kernel(meta, act_a, act_b, *rest):
    sources, outs, (act, gm, acc, block, sems) = rest[:7], rest[7:13], rest[13:]
    feats, frames = act_a.shape
    half = feats // 2
    section = meta[0]
    copies = [
        pltpu.make_async_copy(act_a, act.at[:, pl.ds(0, frames)], sems.at[0]),
        pltpu.make_async_copy(act_b, act.at[:, pl.ds(frames, frames)], sems.at[1]),
    ]
    for copy in copies:
        copy.start()
    for m in range(2):
        for owner in range(4):

            @pl.when(section == owner)
            def _():
                source = sources[0].at[m] if owner == 3 else sources[1 + 2 * owner + m]
                place = gm.at[pl.ds(m * frames, frames)]
                pltpu.make_async_copy(source, place, sems.at[2 + m]).start()

    for m in range(2):
        copies[m].wait()
        pltpu.make_async_copy(sources[1], gm.at[pl.ds(m * frames, frames)], sems.at[2 + m]).wait()
    leaving = []
    for h in range(2):

        def multiply(n, carry):
            r = pl.multiple_of(n * 256, 256)
            acc[pl.ds(r, 256), :] = lax.dot_general(
                act[pl.ds(r, 256), :],
                gm[:, h * half : (h + 1) * half],
                (((1,), (0,)), ((), ())),
                preferred_element_type=F32,
            )
            return carry

        lax.fori_loop(0, feats // 256, multiply, 0)

        def place(b, carry):
            r = pl.multiple_of(b * 48, 16)
            block[h, meta[88 + h * 32 + b]] = acc[pl.ds(r, 48), :].astype(BF16)
            return carry

        lax.fori_loop(0, 32, place, 0, unroll=4)
        for p, (start, size) in enumerate(((0, 8), (8, 8), (16, 16))):
            copy = pltpu.make_async_copy(
                block.at[h, pl.ds(start, size)], outs[h * 3 + p], sems.at[4 + h * 3 + p]
            )
            copy.start()
            leaving.append(copy)
    for copy in leaving:
        copy.wait()


def weight_terms(meta, acts, grads, comes):
    feats, frames = acts[0].shape
    half = feats // 2
    sizes = (8, 8, 16)
    operands = [meta, *acts, grads, *comes]
    return pl.pallas_call(
        weight_kernel,
        in_specs=[SMEM, ANY, ANY, HBM] + [ANY] * len(comes),
        out_specs=[ANY] * 6,
        out_shape=[jax.ShapeDtypeStruct((n, 48, half), BF16) for n in sizes] * 2,
        scratch_shapes=[
            pltpu.VMEM((feats, 2 * frames), BF16),
            pltpu.VMEM((2 * frames, feats), BF16),
            pltpu.VMEM((feats, half), F32),
            pltpu.VMEM((2, 32, 48, half), BF16),
            pltpu.SemaphoreType.DMA((10,)),
        ],
        compiler_params=params(60),
        cost_estimate=cost(8),
    )(*operands)


def tap_kernel(meta, x_ref, mixed_ref, gain_ref, taps, *rest):
    sent, (out, frame_out, hid, held, sems) = rest[:6], rest[6:]
    m = pl.program_id(0)
    section = meta[0]
    length = meta[1 + m]
    frames, feats = x_ref.shape[1:]
    cols = feats // LANES

    @pl.when(m == 0)
    def _():
        out[...] = jnp.zeros_like(out)
        for owner, turns in enumerate(((4, 5), (3, 4), (1, 2), (0, 1))):

            @pl.when(section == owner)
            def _():
                for p in range(2):
                    pltpu.make_async_copy(sent[turns[p]], held.at[p], sems.at[p]).start()

    for c in range(cols):
        hid[c, 0:PAD, :] = jnp.zeros((PAD, LANES), F32)
        hid[c, PAD + frames : 2 * PAD + frames, :] = jnp.zeros((PAD, LANES), F32)

    def load(i, carry):
        r = pl.multiple_of(i * 16, 16)
        keep = r + lax.broadcasted_iota(jnp.int32, (16, LANES), 0) < length
        for c in range(cols):
            v = x_ref[0, pl.ds(r, 16), c * LANES : (c + 1) * LANES].astype(F32)
            hid[c, pl.ds(r + PAD, 16), :] = jnp.where(keep, v, 0.0)
        return carry

    lax.fori_loop(0, frames // 16, load, 0, unroll=2)
    for c in range(cols):
        span = slice(c * LANES, (c + 1) * LANES)

        def add(i, sums):
            r = pl.multiple_of(i * 32, 32)
            grown = list(sums)
            wide = mixed_ref[0, pl.ds(r, 32), span].astype(F32)
            for q in range(4):
                g = wide[8 * q : 8 * q + 8]
                for k in range(5):
                    grown[k] = grown[k] + g * hid[c, pl.ds(r + PAD - 2 + k + 8 * q, 8), :]
            return tuple(grown)

        sums = lax.fori_loop(0, frames // 32, add, (jnp.zeros((8, LANES), F32),) * 5)
        for k in range(5):
            out[k : k + 1, span] += jnp.sum(sums[k], axis=0, keepdims=True)
    out[5:6, :] += jnp.sum(gain_ref[0], axis=0, keepdims=True) / taps[5:6, :]
    leave = pltpu.make_async_copy(held, frame_out, sems.at[2])

    @pl.when(m == 0)
    def _():
        for p in range(2):
            pltpu.make_async_copy(sent[0], held.at[p], sems.at[p]).wait()
        leave.start()

    @pl.when(m == 1)
    def _():
        leave.wait()


def tap_terms(meta, x, mixed, gain, taps, sent):
    micro, frames, feats = x.shape
    return pl.pallas_call(
        tap_kernel,
        grid=(micro,),
        in_specs=[
            SMEM,
            pl.BlockSpec((1, frames, feats), lambda m: (m, 0, 0)),
            pl.BlockSpec((1, frames, feats), lambda m: (m, 0, 0)),
            pl.BlockSpec((1, 8, feats), lambda m: (m, 0, 0)),
            pl.BlockSpec(taps.shape, lambda m: (0, 0)),
        ]
        + [HBM] * 6,
        out_specs=[pl.BlockSpec((8, feats), lambda m: (0, 0)), HBM],
        out_shape=[
            jax.ShapeDtypeStruct((8, feats), F32),
            jax.ShapeDtypeStruct(x.shape, BF16),
        ],
        scratch_shapes=[
            pltpu.VMEM((feats // LANES, frames + 2 * PAD, LANES), F32),
            pltpu.VMEM(x.shape, BF16),
            pltpu.SemaphoreType.DMA((3,)),
        ],
        compiler_params=params(60),
        cost_estimate=cost(6),
    )(meta, x, mixed, gain, taps, *sent)


def shift(x, axis, d):
    n = lax.axis_size(axis)
    return lax.ppermute(x, axis, [(i, (i + d) % n) for i in range(n)])


def swap(x, axis, d):
    n = lax.axis_size(axis)
    return lax.ppermute(x, axis, [(i, i ^ d) for i in range(n)])


def gather_weights(shard, small):
    rows, width = shard.shape
    half = width // 2
    extra = jnp.zeros((16, half), BF16).at[0, : small.size].set(small.reshape(-1))
    own = [jnp.concatenate([shard[:, :half], extra]), shard[:, half:]]
    pairs = [jnp.stack([p, swap(p, "xh", 1)]) for p in own]

    def near(p, axis):
        return [p] + [shift(p, axis, d) for d in (1, -1, 2)]

    first = [jnp.concatenate(near(p, a)) for p, a in zip(pairs, ("y", "z"))]
    packed = first[0][:, rows, : small.size]
    packed = jnp.stack(near(packed, "z"))
    packed = packed.reshape(4, 4, 2, *small.shape)
    packed = jnp.stack([packed[i] for i in (0, 2, 3, 1)])
    packed = jnp.stack([packed[:, i] for i in (0, 2, 3, 1)], axis=1)
    x, z, y = (lax.axis_index(a) for a in ("xh", "z", "y"))
    packed = jnp.tile(packed, (2, 2, 2, 1, 1))
    zero = jnp.zeros((), jnp.int32)
    packed = lax.dynamic_slice(
        packed, ((4 - z) % 4, (4 - y) % 4, (2 - x) % 2, zero, zero), (4, 4, 2, *small.shape)
    )
    whole = packed.transpose(3, 2, 0, 1, 4).reshape(small.shape[0], width)

    def ring(own, axis):
        cut = own.shape[0] // 2
        left, right = shift(own, axis, 1), shift(own, axis, -1)
        return own, left, right, shift(left[:cut], axis, 1), shift(right[cut:], axis, -1)

    pieces = [ring(p[:, :rows], a) for p, a in zip(first, ("z", "y"))]
    return [*pieces[0], *pieces[1]], whole


def scatter_near(pieces, axis):
    total = pieces[0]
    for d in (1, 2, 3):
        total = total + shift(pieces[d].astype(BF16), axis, d).astype(F32)
    return total


def scatter_weights(parts, terms):
    rings = (parts[:3], "z"), (parts[3:], "y")
    moved = [(shift(p[0], a, 1), shift(p[1], a, -1)) for p, a in rings]
    moved, terms = lax.optimization_barrier((moved, terms))
    halves = []
    for (parts_, axis), (p, q) in zip(rings, moved):
        kept = parts_[2]
        n = kept.shape[0] // 4
        up_a, dn_b, own_a, own_b = (kept[i * n : (i + 1) * n].astype(F32) for i in range(4))
        far_p = shift((up_a + p[:n].astype(F32)).astype(BF16), axis, 1)
        far_q = shift((dn_b + q[:n].astype(F32)).astype(BF16), axis, -1)
        a = own_a + far_p.astype(F32) + q[n:].astype(F32)
        b = own_b + far_q.astype(F32) + p[n:].astype(F32)
        halves.append(jnp.concatenate([a, b]))
    a, b = halves
    packed = scatter_near(terms, "z")
    extra = jnp.zeros((8, 16, a.shape[2]), F32).at[:, 0, : packed.shape[1]].set(packed)
    a = jnp.concatenate([a, extra], axis=1)
    own = []
    for blocks, axis in ((a, "y"), (b, "z")):
        pieces = [
            jnp.stack([blocks[SCATTERED.index((i, r))] for r in range(2)]) for i in range(4)
        ]
        summed = scatter_near(pieces, axis)
        own.append(summed[0] + swap(summed[1].astype(BF16), "xh", 1).astype(F32))
    rows = own[1].shape[0]
    return jnp.concatenate([own[0][:rows], own[1]], axis=1), own[0][rows, : packed.shape[1]]


def body(saved_inputs, grad_outputs, lengths, pointwise, depth_kernel, norm_gain):
    section = lax.axis_index("section")
    x, z, y = (lax.axis_index(a) for a in ("xh", "z", "y"))
    inputs = saved_inputs[0, :, 0]
    grads = grad_outputs[:, 0]
    lens = lengths[:, 0]
    micro, frames, features = inputs.shape
    factor = float(32 * micro * frames) ** (-0.5)

    gather_table, scatter_table = tables()
    table = jnp.asarray(np.concatenate([gather_table, scatter_table], axis=-1).reshape(32, -1))
    table = lax.dynamic_index_in_dim(table, x * 16 + z * 4 + y, 0, keepdims=False)
    meta = jnp.concatenate([section[None], lens, jnp.zeros((5,), jnp.int32), table])

    small = jnp.concatenate([depth_kernel[0], norm_gain[0:1]], axis=0)
    weights, small = gather_weights(pointwise[0], small)
    taps = jnp.pad(small.astype(F32), ((0, 2), (0, 0)))
    made = [forward(m, lens, inputs, taps) for m in range(2)]
    saved = [made[m][i] for i in range(3) for m in range(2)]
    acts = [made[m][3] for m in range(2)]

    def turn(state, come, come_one, who):
        return relay(who, meta, grads, come, come_one, weights, saved, taps, state)

    def hop(block, source):
        return lax.ppermute(block, "section", [(source, source - 1)])

    outs = [None] * 6
    outs[0], state = turn(None, saved[0], saved[0], (-1, -1, -1, 0))
    two_0 = hop(outs[0], 3)
    outs[1], state = turn(state, two_0, two_0, (-1, -1, 0, 1))
    two_1, one_0 = hop(outs[1], 3), hop(outs[1], 2)
    outs[2], state = turn(state, two_1, two_1, (-1, -1, 1, -1))
    one_1 = hop(outs[2], 2)
    outs[3], state = turn(state, one_0, one_0, (-1, 0, -1, -1))
    outs[3], one_1 = lax.optimization_barrier((outs[3], one_1))
    zero_0 = hop(outs[3], 1)
    outs[4], state = turn(state, zero_0, one_1, (0, 1, -1, -1))
    zero_1 = hop(outs[4], 1)
    parts = weight_terms(meta, acts, grads, [zero_0, zero_1, one_0, one_1, two_0, two_1])
    outs[5], (mixed, gain) = turn(state, zero_1, zero_1, (1, -1, -1, -1))
    sums, frame_out = tap_terms(meta, inputs, mixed, gain, taps, outs)

    def terms():
        blocks = (sums[:6] * factor).reshape(6, 2, 4, 4, 48)
        blocks = blocks.transpose(2, 3, 1, 0, 4).reshape(4, 4, 2, 288)
        blocks = lax.dynamic_slice(
            jnp.tile(blocks, (2, 2, 2, 1)), (z, y, x, jnp.zeros((), jnp.int32)), (4, 4, 2, 288)
        )
        return jnp.stack([blocks[:, i, r] for i, r in SCATTERED], axis=1)

    point_share, share = scatter_weights(parts, terms())
    share = share.reshape(6, 48)
    return (
        frame_out[None, :, None],
        (point_share * factor)[None],
        share[None, :5],
        share[5:6],
    )


def solution(mesh):
    fine = Mesh(mesh.devices.reshape(4, 2, 4, 4), ("section", "xh", "z", "y"))
    fsdp = ("xh", "z", "y")
    return jax.shard_map(
        body,
        mesh=fine,
        in_specs=(
            P("section", None, fsdp, None, None),
            P(None, fsdp, None, None),
            P(None, fsdp),
            P("section", fsdp, None),
            P("section", None, fsdp),
            P("section", fsdp),
        ),
        out_specs=(
            P("section", None, fsdp, None, None),
            P("section", fsdp, None),
            P("section", None, fsdp),
            P("section", fsdp),
        ),
        check_vma=False,
    )
```

time: 311 us -> 255 us (0.82)
  waiting for transfers between devices: 117 us -> 79.9 us
  local copies, waits for them, and re-layouts: 55.3 us -> 24.5 us
  Pallas kernels: 58 us -> 70.9 us
  other arithmetic: 3.36 us -> 10.3 us
  between operations: 7.89 us -> 1.49 us
    unnamed x95 -> x47, local copies, waits for them, and re-layouts: 41.9 us -> 10.2 us
    ppermute x12 -> x4, waiting for transfers between devices: 30.3 us -> 5.89 us  [swap(): return lax.ppermute(x, axis, [(i, i ^ d) for i in range(n)])]
    pallas_call x7 -> x9, Pallas kernels: 52.6 us -> 62.5 us  [the longest x6 29.9 us: relay(): pl.pallas_call(functools.partial(relay_kernel, first, who), in_specs=spec...]
    ppermute x32 -> x34, starting transfers between devices: 42.1 us -> 51.4 us  [shift(): return lax.ppermute(x, axis, [(i, (i + d) % n) for i in range(n)])]
    ppermute x12 -> x4, starting transfers between devices: 18.6 us -> 9.51 us  [swap(): return lax.ppermute(x, axis, [(i, i ^ d) for i in range(n)])]
    ppermute x4 -> x6, waiting for transfers between devices: 67.9 us -> 60 us  [hop(): return lax.ppermute(block, 'section', [(source, source - 1)])]
    concatenate x8 -> x3, local copies, waits for them, and re-layouts: 5.33 us -> 0.04 us  [the longest x2 0.03 us: gather_weights(): first = [jnp.concatenate(near(p, a)) for p, a in zip(pairs, ('y', 'z'))]]
    ppermute x32 -> x34, waiting for transfers between devices: 19.1 us -> 14 us  [shift(): return lax.ppermute(x, axis, [(i, (i + d) % n) for i in range(n)])]
  transfers between devices with their start and end apart: 48 -> 44, of which waited for: 21 -> 10; matrix products, arithmetic and copies ran while one was open for 7% -> 9% of each run, Pallas kernels for 10% -> 17%
where the time goes in v2:
time: 255 us; the launch traced here: 254 us
  waiting for transfers between devices  79.9 us (31%)
  Pallas kernels  70.9 us (28%)
  starting transfers between devices  66.6 us (26%)
  local copies, waits for them, and re-layouts  24.5 us (10%)
  other arithmetic  10.3 us (4%)
    ppermute x6, waiting for transfers between devices, hop(): return lax.ppermute(block, 'section', [(source, source - 1)])  60 us
    ppermute x34, starting transfers between devices, shift(): return lax.ppermute(x, axis, [(i, (i + d) % n) for i in range(n)])  51.4 us
    pallas_call x6, Pallas kernels, relay(): pl.pallas_call(functools.partial(relay_kernel, first, who), in_specs=spec...  29.9 us
    pallas_call x2, Pallas kernels, forward(): pl.pallas_call(functools.partial(forward_kernel, m), in_specs=[SMEM, HBM,...  20.1 us
    ppermute x34, waiting for transfers between devices, shift(): return lax.ppermute(x, axis, [(i, (i + d) % n) for i in range(n)])  14 us
    pallas_call x1, Pallas kernels, weight_terms(): pl.pallas_call(weight_kernel, in_specs=[SMEM, ANY, ANY, HBM] + [ANY] * le...  12.5 us
    unnamed x47, local copies, waits for them, and re-layouts  10.2 us
    ppermute x4, starting transfers between devices, swap(): return lax.ppermute(x, axis, [(i, i ^ d) for i in range(n)])  9.51 us
  transfers between devices with their start and end apart: 44, of which 10 were waited for; matrix products, arithmetic and copies ran while one was open for 9% of the time, Pallas kernels for 17%

profile of v2, /device:TPU:0, one launch (start us, length us, event | category | flops | bytes accessed | tf_op | source)
XLA Modules:
  0.0 253.7 jit_solution(6496967167695336638)
XLA Ops:
  2.4 3.2 %collective-permute-start = (bf16[64,768]{1,0:T(8,128)(2,1)S(1)}, bf16[64,768]{1,0:T(8,128)(2,1)S(1)}, u32[]{:S(2)}, u32[]{:S(2)}) collective-permute-start(bf16[64,768]{1,0:T(8,128)(2,1)S(1)} %get-tuple-element.150), channel_id=1, source_target_pairs={{0,16},{16,0},{1,17},{17,1},{2,18},{18,2},{3,19},{19,3},{4,20},{20... | collective-permute-start | bytes 294920 | tf_op jit(solution)/shard_map/ppermute | solution.py:504
  9.0 2.5 collective-permute-done.11
  20.8 2.6 %collective-permute-start.3 = (bf16[2,64,768]{2,1,0:T(8,128)(2,1)S(1)}, bf16[2,64,768]{2,1,0:T(8,128)(2,1)S(1)}, u32[]{:S(2)}, u32[]{:S(2)}) collective-permute-start(bf16[2,64,768]{2,1,0:T(8,128)(2,1)S(1)} %pad_maximum_fusion), channel_id=1, source_target_pairs={{0,2},{1,3},{2,0},{3,1},{4,6},{5,7},{6,4},{7,5},{8,10},{9,11},{10,... | collective-permute-start | bytes 589832 | tf_op jit(solution)/shard_map/ppermute | solution.py:499
  29.1 2.6 %collective-permute-done.3 = bf16[2,64,768]{2,1,0:T(8,128)(2,1)S(1)} collective-permute-done((bf16[2,64,768]{2,1,0:T(8,128)(2,1)S(1)}, bf16[2,64,768]{2,1,0:T(8,128)(2,1)S(1)}, u32[]{:S(2)}, u32[]{:S(2)}) %collective-permute-start.3) | collective-permute-done | bytes 196640 | tf_op jit(solution)/shard_map/ppermute | solution.py:499
  32.4 3.4 %collective-permute-start.5 = (bf16[8,288]{1,0:T(8,128)(2,1)}, bf16[8,288]{1,0:T(8,128)(2,1)}, u32[]{:S(2)}, u32[]{:S(2)}) collective-permute-start(bf16[8,288]{1,0:T(8,128)(2,1)} %bitcast.76), channel_id=1, source_target_pairs={{0,8},{4,12},{8,0},{12,4},{1,9},{5,13},{9,1},{13,5},{2,10},{6,14},... | collective-permute-start | bytes 13832 | tf_op jit(solution)/shard_map/ppermute | solution.py:499
  36.6 3.2 %collective-permute-start.8 = (bf16[8,48,768]{2,1,0:T(8,128)(2,1)S(1)}, bf16[8,48,768]{2,1,0:T(8,128)(2,1)S(1)}, u32[]{:S(2)}, u32[]{:S(2)}) collective-permute-start(bf16[8,48,768]{2,1,0:T(8,128)(2,1)S(1)} %slice.330.rest_0_), channel_id=1, source_target_pairs={{0,12},{4,0},{8,4},{12,8},{1,13},{5,1},{9,5},{13,9},{2,14},{6,2},{... | collective-permute-start | bytes 1769480 | tf_op jit(solution)/shard_map/ppermute | solution.py:499
  48.6 10.1 %shard_map.102 = (bf16[512,1536]{1,0:T(8,128)(2,1)}, bf16[512,1536]{1,0:T(8,128)(2,1)}, f32[512,128]{1,0:T(8,128)}, bf16[1536,512]{1,0:T(8,128)(2,1)}) custom-call(s32[2]{0:T(128)} %bitcast.93, bf16[2,512,1536]{2,1,0:T(8,128)(2,1)} %bitcast.95, f32[8,1536]{1,0:T(8,128)} %pad_convert_fusion.taps.rest_16_), custom_call_target="tpu_custom_call" | custom-call | flops 8000000000 | bytes 1048576 | tf_op jit(solution)/shard_map/pallas_call | solution.py:119
  64.3 3.2 %collective-permute-start.10 = (bf16[4,48,768]{2,1,0:T(8,128)(2,1)}, bf16[4,48,768]{2,1,0:T(8,128)(2,1)S(1)}, u32[]{:S(2)}, u32[]{:S(2)}) collective-permute-start(bf16[4,48,768]{2,1,0:T(8,128)(2,1)} %slice.332), channel_id=1, source_target_pairs={{0,12},{4,0},{8,4},{12,8},{1,13},{5,1},{9,5},{13,9},{2,14},{6,2},{... | collective-permute-start | bytes 884744 | tf_op jit(solution)/shard_map/ppermute | solution.py:499
  67.6 10.1 %shard_map.103 = (bf16[512,1536]{1,0:T(8,128)(2,1)}, bf16[512,1536]{1,0:T(8,128)(2,1)}, f32[512,128]{1,0:T(8,128)}, bf16[1536,512]{1,0:T(8,128)(2,1)}) custom-call(s32[2]{0:T(128)} %bitcast.94, bf16[2,512,1536]{2,1,0:T(8,128)(2,1)} %bitcast.96, f32[8,1536]{1,0:T(8,128)} %pad_convert_fusion.taps.rest_16_), custom_call_target="tpu_custom_call" | custom-call | flops 8000000000 | bytes 1048576 | tf_op jit(solution)/shard_map/pallas_call | solution.py:119
  90.7 55.8 %collective-permute-done.23.come.rest_1_ = bf16[512,1536]{1,0:T(8,128)(2,1)S(1)} collective-permute-done((bf16[512,1536]{1,0:T(8,128)(2,1)}, bf16[512,1536]{1,0:T(8,128)(2,1)S(1)}, u32[]{:S(2)}, u32[]{:S(2)}) %collective-permute-start.23) | collective-permute-done | bytes 1572896 | tf_op jit(solution)/shard_map/ppermute | solution.py:601
  147.7 13.0 %shard_map.108 = (bf16[512,1536]{1,0:T(8,128)(2,1)}, bf16[2,512,1536]{2,1,0:T(8,128)(2,1)}, f32[2,8,1536]{2,1,0:T(8,128)}) custom-call(s32[152]{0:T(256)} %pad_add_fusion.meta, bf16[2,512,1536]{2,1,0:T(8,128)(2,1)} %bitcast.81, bf16[512,1536]{1,0:T(8,128)(2,1)} %copy-done.15, ...), custom_call_target="tpu_custom_call", output_to_operand_aliasing={{1}: (21, {}), {2}: (22, {})} | custom-call | flops 1000000000 | bytes 1048576 | tf_op jit(solution)/shard_map/pallas_call | solution.py:307
  162.0 4.2 %collective-permute-done.24.come.come_one.rest_2_ = bf16[512,1536]{1,0:T(8,128)(2,1)S(1)} collective-permute-done((bf16[512,1536]{1,0:T(8,128)(2,1)}, bf16[512,1536]{1,0:T(8,128)(2,1)S(1)}, u32[]{:S(2)}, u32[]{:S(2)}) %collective-permute-start.24) | collective-permute-done | bytes 1572896 | tf_op jit(solution)/shard_map/ppermute | solution.py:601
  167.3 12.5 %shard_map.111 = (bf16[8,48,768]{2,1,0:T(8,128)(2,1)}, bf16[8,48,768]{2,1,0:T(8,128)(2,1)}, bf16[16,48,768]{2,1,0:T(8,128)(2,1)}, bf16[8,48,768]{2,1,0:T(8,128)(...) custom-call(s32[152]{0:T(256)} %pad_add_fusion.meta, bf16[1536,512]{1,0:T(8,128)(2,1)} %get-tuple-element.96.act_a, ...), custom_call_target="tpu_custom_call" | custom-call | flops 8000000000 | bytes 1048576 | tf_op jit(solution)/shard_map/pallas_call | solution.py:391
  179.9 3.2 %collective-permute-start.26 = (bf16[8,48,768]{2,1,0:T(8,128)(2,1)}, bf16[8,48,768]{2,1,0:T(8,128)(2,1)}, u32[]{:S(2)}, u32[]{:S(2)}) collective-permute-start(bf16[8,48,768]{2,1,0:T(8,128)(2,1)} %get-tuple-element.100), channel_id=1, source_target_pairs={{0,12},{4,0},{8,4},{12,8},{1,13},{5,1},{9,5},{13,9},{2,14},{6,2},{... | collective-permute-start | bytes 1769480 | tf_op jit(solution)/shard_map/ppermute | solution.py:499
  183.1 3.2 %collective-permute-start.28 = (bf16[8,48,768]{2,1,0:T(8,128)(2,1)}, bf16[8,48,768]{2,1,0:T(8,128)(2,1)}, u32[]{:S(2)}, u32[]{:S(2)}) collective-permute-start(bf16[8,48,768]{2,1,0:T(8,128)(2,1)} %get-tuple-element.102), channel_id=1, source_target_pairs={{0,3},{1,0},{2,1},{3,2},{4,7},{5,4},{6,5},{7,6},{8,11},{9,8},{10,9... | collective-permute-start | bytes 1769480 | tf_op jit(solution)/shard_map/ppermute | solution.py:499
  186.4 13.1 %shard_map.109 = (bf16[512,1536]{1,0:T(8,128)(2,1)}, bf16[2,512,1536]{2,1,0:T(8,128)(2,1)}, f32[2,8,1536]{2,1,0:T(8,128)}) custom-call(s32[152]{0:T(256)} %pad_add_fusion.meta, bf16[2,512,1536]{2,1,0:T(8,128)(2,1)} %bitcast.83, bf16[512,1536]{1,0:T(8,128)(2,1)} %copy-done.13, ...), custom_call_target="tpu_custom_call", output_to_operand_aliasing={{1}: (21, {}), {2}: (22, {})} | custom-call | flops 1000000000 | bytes 1048576 | tf_op jit(solution)/shard_map/pallas_call | solution.py:307
  199.4 8.4 %shard_map.110 = (f32[8,1536]{1,0:T(8,128)}, bf16[2,512,1536]{2,1,0:T(8,128)(2,1)}) custom-call(s32[152]{0:T(256)} %pad_add_fusion.meta, bf16[2,512,1536]{2,1,0:T(8,128)(2,1)} %bitcast.97, bf16[2,512,1536]{2,1,0:T(8,128)(2,1)} %get-tuple-element.92.mixed_ref, f32[2,8,1536]{2,1,0:T(8,128)} %get-tuple-element.93.gain_ref, ...), custom_call_target="tpu_custom_call" | custom-call | flops 6000000000 | bytes 1048576 | tf_op jit(solution)/shard_map/pallas_call | solution.py:471
  213.6 3.7 %collective-permute-start.32 = (bf16[8,288]{1,0:T(8,128)(2,1)S(1)}, bf16[8,288]{1,0:T(8,128)(2,1)S(1)}, u32[]{:S(2)}, u32[]{:S(2)}) collective-permute-start(bf16[8,288]{1,0:T(8,128)(2,1)S(1)} %get-tuple-element.155), channel_id=1, source_target_pairs={{0,8},{4,12},{8,0},{12,4},{1,9},{5,13},{9,1},{13,5},{2,10},{6,14},... | collective-permute-start | bytes 13832 | tf_op jit(solution)/shard_map/ppermute | solution.py:499
  218.4 3.7 %collective-permute-done.31 = bf16[8,288]{1,0:T(8,128)(2,1)S(1)} collective-permute-done((bf16[8,288]{1,0:T(8,128)(2,1)S(1)}, bf16[8,288]{1,0:T(8,128)(2,1)S(1)}, u32[]{:S(2)}, u32[]{:S(2)}) %collective-permute-start.31) | collective-permute-done | bytes 4640 | tf_op jit(solution)/shard_map/ppermute | solution.py:499
  224.4 3.1 %collective-permute-done.39 = bf16[4,48,768]{2,1,0:T(8,128)(2,1)S(1)} collective-permute-done((bf16[4,48,768]{2,1,0:T(8,128)(2,1)S(1)}, bf16[4,48,768]{2,1,0:T(8,128)(2,1)S(1)}, u32[]{:S(2)}, u32[]{:S(2)}) %collective-permute-start.39) | collective-permute-done | bytes 294944 | tf_op jit(solution)/shard_map/ppermute | solution.py:499
  236.2 2.9 %collective-permute-start.42 = (bf16[2,48,768]{2,1,0:T(8,128)(2,1)S(1)}, bf16[2,48,768]{2,1,0:T(8,128)(2,1)S(1)}, u32[]{:S(2)}, u32[]{:S(2)}) collective-permute-start(bf16[2,48,768]{2,1,0:T(8,128)(2,1)S(1)} %pad_maximum_fusion.7), channel_id=1, source_target_pairs={{0,12},{4,0},{8,4},{12,8},{1,13},{5,1},{9,5},{13,9},{2,14},{6,2},{... | collective-permute-start | bytes 442376 | tf_op jit(solution)/shard_map/ppermute | solution.py:499
  242.2 3.1 %collective-permute-start.43 = (bf16[48,768]{1,0:T(8,128)(2,1)S(1)}, bf16[48,768]{1,0:T(8,128)(2,1)S(1)}, u32[]{:S(2)}, u32[]{:S(2)}) collective-permute-start(bf16[48,768]{1,0:T(8,128)(2,1)S(1)} %fusion.10), channel_id=1, source_target_pairs={{0,16},{16,0},{1,17},{17,1},{2,18},{18,2},{3,19},{19,3},{4,20},{20... | collective-permute-start | bytes 221192 | tf_op jit(solution)/shard_map/ppermute | solution.py:504
  245.5 2.8 %collective-permute-start.37 = (bf16[64,768]{1,0:T(8,128)(2,1)S(1)}, bf16[64,768]{1,0:T(8,128)(2,1)S(1)}, u32[]{:S(2)}, u32[]{:S(2)}) collective-permute-start(bf16[64,768]{1,0:T(8,128)(2,1)S(1)} %fusion.9), channel_id=1, source_target_pairs={{0,16},{16,0},{1,17},{17,1},{2,18},{18,2},{3,19},{19,3},{4,20},{20... | collective-permute-start | bytes 294920 | tf_op jit(solution)/shard_map/ppermute | solution.py:504
  248.3 3.4 %collective-permute-done.37 = bf16[64,768]{1,0:T(8,128)(2,1)S(1)} collective-permute-done((bf16[64,768]{1,0:T(8,128)(2,1)S(1)}, bf16[64,768]{1,0:T(8,128)(2,1)S(1)}, u32[]{:S(2)}, u32[]{:S(2)}) %collective-permute-start.37) | collective-permute-done | bytes 98336 | tf_op jit(solution)/shard_map/ppermute | solution.py:504
  (193 shorter events, 75.4 us)
Async XLA Ops:
  2.4 15.0 %collective-permute-start = (bf16[64,768]{1,0:T(8,128)(2,1)S(1)}, bf16[64,768]{1,0:T(8,128)(2,1)S(1)}, u32[]{:S(2)}, u32[]{:S(2)}) collective-permute-start(bf16[64,768]{1,0:T(8,128)(2,1)S(1)} %get-tuple-element.150), channel_id=1, source_target_pairs={{0,16},{16,0},{1,17},{17,1},{2,18},{18,2},{3,19},{19,3},{4,20},{20... | collective-permute-start | bytes 294920 | tf_op jit(solution)/shard_map/ppermute | solution.py:504
  11.5 9.3 %collective-permute-start.12 = (bf16[2,48,768]{2,1,0:T(8,128)(2,1)S(1)}, bf16[2,48,768]{2,1,0:T(8,128)(2,1)S(1)}, u32[]{:S(2)}, u32[]{:S(2)}) collective-permute-start(bf16[2,48,768]{2,1,0:T(8,128)(2,1)S(1)} %pad_maximum_fusion.4), channel_id=1, source_target_pairs={{0,4},{4,8},{8,12},{12,0},{1,5},{5,9},{9,13},{13,1},{2,6},{6,10},{... | collective-permute-start | bytes 442376 | tf_op jit(solution)/shard_map/ppermute | solution.py:499
  13.4 9.9 %collective-permute-start.13 = (bf16[2,48,768]{2,1,0:T(8,128)(2,1)S(1)}, bf16[2,48,768]{2,1,0:T(8,128)(2,1)S(1)}, u32[]{:S(2)}, u32[]{:S(2)}) collective-permute-start(bf16[2,48,768]{2,1,0:T(8,128)(2,1)S(1)} %pad_maximum_fusion.4), channel_id=1, source_target_pairs={{0,12},{4,0},{8,4},{12,8},{1,13},{5,1},{9,5},{13,9},{2,14},{6,2},{... | collective-permute-start | bytes 442376 | tf_op jit(solution)/shard_map/ppermute | solution.py:499
  17.5 11.6 %collective-permute-start.1 = (bf16[2,64,768]{2,1,0:T(8,128)(2,1)S(1)}, bf16[2,64,768]{2,1,0:T(8,128)(2,1)S(1)}, u32[]{:S(2)}, u32[]{:S(2)}) collective-permute-start(bf16[2,64,768]{2,1,0:T(8,128)(2,1)S(1)} %pad_maximum_fusion), channel_id=1, source_target_pairs={{0,1},{1,2},{2,3},{3,0},{4,5},{5,6},{6,7},{7,4},{8,9},{9,10},{10,1... | collective-permute-start | bytes 589832 | tf_op jit(solution)/shard_map/ppermute | solution.py:499
  19.1 10.0 %collective-permute-start.2 = (bf16[2,64,768]{2,1,0:T(8,128)(2,1)S(1)}, bf16[2,64,768]{2,1,0:T(8,128)(2,1)S(1)}, u32[]{:S(2)}, u32[]{:S(2)}) collective-permute-start(bf16[2,64,768]{2,1,0:T(8,128)(2,1)S(1)} %pad_maximum_fusion), channel_id=1, source_target_pairs={{0,3},{1,0},{2,1},{3,2},{4,7},{5,4},{6,5},{7,6},{8,11},{9,8},{10,9... | collective-permute-start | bytes 589832 | tf_op jit(solution)/shard_map/ppermute | solution.py:499
  20.8 11.0 %collective-permute-start.3 = (bf16[2,64,768]{2,1,0:T(8,128)(2,1)S(1)}, bf16[2,64,768]{2,1,0:T(8,128)(2,1)S(1)}, u32[]{:S(2)}, u32[]{:S(2)}) collective-permute-start(bf16[2,64,768]{2,1,0:T(8,128)(2,1)S(1)} %pad_maximum_fusion), channel_id=1, source_target_pairs={{0,2},{1,3},{2,0},{3,1},{4,6},{5,7},{6,4},{7,5},{8,10},{9,11},{10,... | collective-permute-start | bytes 589832 | tf_op jit(solution)/shard_map/ppermute | solution.py:499
  23.4 35.2 %collective-permute-start.15 = (bf16[8,48,768]{2,1,0:T(8,128)(2,1)S(1)}, bf16[8,48,768]{2,1,0:T(8,128)(2,1)S(1)}, u32[]{:S(2)}, u32[]{:S(2)}) collective-permute-start(bf16[8,48,768]{2,1,0:T(8,128)(2,1)S(1)} %constant_dynamic-update-slice_fusion.9.rest_5_), channel_id=1, source_target_pairs={{0,1},{1,2},{2,3},{3,0},{4,5},{5,6},{6,7},{7,4},{8,9},{9,10},{10,1... | collective-permute-start | bytes 1769480 | tf_op jit(solution)/shard_map/ppermute | solution.py:499
  24.3 36.6 %collective-permute-start.16 = (bf16[8,48,768]{2,1,0:T(8,128)(2,1)S(1)}, bf16[8,48,768]{2,1,0:T(8,128)(2,1)S(1)}, u32[]{:S(2)}, u32[]{:S(2)}) collective-permute-start(bf16[8,48,768]{2,1,0:T(8,128)(2,1)S(1)} %constant_dynamic-update-slice_fusion.9.rest_5_), channel_id=1, source_target_pairs={{0,3},{1,0},{2,1},{3,2},{4,7},{5,4},{6,5},{7,6},{8,11},{9,8},{10,9... | collective-permute-start | bytes 1769480 | tf_op jit(solution)/shard_map/ppermute | solution.py:499
  36.6 26.8 %collective-permute-start.8 = (bf16[8,48,768]{2,1,0:T(8,128)(2,1)S(1)}, bf16[8,48,768]{2,1,0:T(8,128)(2,1)S(1)}, u32[]{:S(2)}, u32[]{:S(2)}) collective-permute-start(bf16[8,48,768]{2,1,0:T(8,128)(2,1)S(1)} %slice.330.rest_0_), channel_id=1, source_target_pairs={{0,12},{4,0},{8,4},{12,8},{1,13},{5,1},{9,5},{13,9},{2,14},{6,2},{... | collective-permute-start | bytes 1769480 | tf_op jit(solution)/shard_map/ppermute | solution.py:499
  40.6 27.0 %collective-permute-start.7 = (bf16[8,48,768]{2,1,0:T(8,128)(2,1)S(1)}, bf16[8,48,768]{2,1,0:T(8,128)(2,1)S(1)}, u32[]{:S(2)}, u32[]{:S(2)}) collective-permute-start(bf16[8,48,768]{2,1,0:T(8,128)(2,1)S(1)} %slice.330.rest_0_), channel_id=1, source_target_pairs={{0,4},{4,8},{8,12},{12,0},{1,5},{5,9},{9,13},{13,1},{2,6},{6,10},{... | collective-permute-start | bytes 1769480 | tf_op jit(solution)/shard_map/ppermute | solution.py:499
  59.5 18.3 %collective-permute-start.17 = (bf16[4,48,768]{2,1,0:T(8,128)(2,1)}, bf16[4,48,768]{2,1,0:T(8,128)(2,1)S(1)}, u32[]{:S(2)}, u32[]{:S(2)}) collective-permute-start(bf16[4,48,768]{2,1,0:T(8,128)(2,1)} %slice.334), channel_id=1, source_target_pairs={{0,1},{1,2},{2,3},{3,0},{4,5},{5,6},{6,7},{7,4},{8,9},{9,10},{10,1... | collective-permute-start | bytes 884744 | tf_op jit(solution)/shard_map/ppermute | solution.py:499
  61.7 16.1 %collective-permute-start.18 = (bf16[4,48,768]{2,1,0:T(8,128)(2,1)}, bf16[4,48,768]{2,1,0:T(8,128)(2,1)S(1)}, u32[]{:S(2)}, u32[]{:S(2)}) collective-permute-start(bf16[4,48,768]{2,1,0:T(8,128)(2,1)} %slice.335), channel_id=1, source_target_pairs={{0,3},{1,0},{2,1},{3,2},{4,7},{5,4},{6,5},{7,6},{8,11},{9,8},{10,9... | collective-permute-start | bytes 884744 | tf_op jit(solution)/shard_map/ppermute | solution.py:499
  64.3 13.5 %collective-permute-start.10 = (bf16[4,48,768]{2,1,0:T(8,128)(2,1)}, bf16[4,48,768]{2,1,0:T(8,128)(2,1)S(1)}, u32[]{:S(2)}, u32[]{:S(2)}) collective-permute-start(bf16[4,48,768]{2,1,0:T(8,128)(2,1)} %slice.332), channel_id=1, source_target_pairs={{0,12},{4,0},{8,4},{12,8},{1,13},{5,1},{9,5},{13,9},{2,14},{6,2},{... | collective-permute-start | bytes 884744 | tf_op jit(solution)/shard_map/ppermute | solution.py:499
  67.6 10.3 %collective-permute-start.9 = (bf16[4,48,768]{2,1,0:T(8,128)(2,1)S(1)}, bf16[4,48,768]{2,1,0:T(8,128)(2,1)S(1)}, u32[]{:S(2)}, u32[]{:S(2)}) collective-permute-start(bf16[4,48,768]{2,1,0:T(8,128)(2,1)S(1)} %slice.331), channel_id=1, source_target_pairs={{0,4},{4,8},{8,12},{12,0},{1,5},{5,9},{9,13},{13,1},{2,6},{6,10},{... | collective-permute-start | bytes 884744 | tf_op jit(solution)/shard_map/ppermute | solution.py:499
  89.4 57.1 %collective-permute-start.23 = (bf16[512,1536]{1,0:T(8,128)(2,1)}, bf16[512,1536]{1,0:T(8,128)(2,1)S(1)}, u32[]{:S(2)}, u32[]{:S(2)}) collective-permute-start(bf16[512,1536]{1,0:T(8,128)(2,1)} %get-tuple-element.85.rest_3_), channel_id=1, source_target_pairs={{32,0},{33,1},{34,2},{35,3},{36,4},{37,5},{38,6},{39,7},{40,8},{41... | collective-permute-start | bytes 4718600 | tf_op jit(solution)/shard_map/ppermute | solution.py:601
  179.8 31.5 %collective-permute-start.25 = (bf16[8,48,768]{2,1,0:T(8,128)(2,1)}, bf16[8,48,768]{2,1,0:T(8,128)(2,1)}, u32[]{:S(2)}, u32[]{:S(2)}) collective-permute-start(bf16[8,48,768]{2,1,0:T(8,128)(2,1)} %get-tuple-element.99), channel_id=1, source_target_pairs={{0,4},{4,8},{8,12},{12,0},{1,5},{5,9},{9,13},{13,1},{2,6},{6,10},{... | collective-permute-start | bytes 1769480 | tf_op jit(solution)/shard_map/ppermute | solution.py:499
  179.9 31.4 %collective-permute-start.26 = (bf16[8,48,768]{2,1,0:T(8,128)(2,1)}, bf16[8,48,768]{2,1,0:T(8,128)(2,1)}, u32[]{:S(2)}, u32[]{:S(2)}) collective-permute-start(bf16[8,48,768]{2,1,0:T(8,128)(2,1)} %get-tuple-element.100), channel_id=1, source_target_pairs={{0,12},{4,0},{8,4},{12,8},{1,13},{5,1},{9,5},{13,9},{2,14},{6,2},{... | collective-permute-start | bytes 1769480 | tf_op jit(solution)/shard_map/ppermute | solution.py:499
  183.1 28.2 %collective-permute-start.27 = (bf16[8,48,768]{2,1,0:T(8,128)(2,1)}, bf16[8,48,768]{2,1,0:T(8,128)(2,1)S(1)}, u32[]{:S(2)}, u32[]{:S(2)}) collective-permute-start(bf16[8,48,768]{2,1,0:T(8,128)(2,1)} %get-tuple-element.101), channel_id=1, source_target_pairs={{0,1},{1,2},{2,3},{3,0},{4,5},{5,6},{6,7},{7,4},{8,9},{9,10},{10,1... | collective-permute-start | bytes 1769480 | tf_op jit(solution)/shard_map/ppermute | solution.py:499
  183.1 28.2 %collective-permute-start.28 = (bf16[8,48,768]{2,1,0:T(8,128)(2,1)}, bf16[8,48,768]{2,1,0:T(8,128)(2,1)}, u32[]{:S(2)}, u32[]{:S(2)}) collective-permute-start(bf16[8,48,768]{2,1,0:T(8,128)(2,1)} %get-tuple-element.102), channel_id=1, source_target_pairs={{0,3},{1,0},{2,1},{3,2},{4,7},{5,4},{6,5},{7,6},{8,11},{9,8},{10,9... | collective-permute-start | bytes 1769480 | tf_op jit(solution)/shard_map/ppermute | solution.py:499
  212.4 9.8 %collective-permute-start.29 = (bf16[4,48,768]{2,1,0:T(8,128)(2,1)S(1)}, bf16[4,48,768]{2,1,0:T(8,128)(2,1)S(1)}, u32[]{:S(2)}, u32[]{:S(2)}) collective-permute-start(bf16[4,48,768]{2,1,0:T(8,128)(2,1)S(1)} %add_convert_fusion.4), channel_id=1, source_target_pairs={{0,4},{4,8},{8,12},{12,0},{1,5},{5,9},{9,13},{13,1},{2,6},{6,10},{... | collective-permute-start | bytes 884744 | tf_op jit(solution)/shard_map/ppermute | solution.py:499
  212.5 9.6 %collective-permute-start.31 = (bf16[8,288]{1,0:T(8,128)(2,1)S(1)}, bf16[8,288]{1,0:T(8,128)(2,1)S(1)}, u32[]{:S(2)}, u32[]{:S(2)}) collective-permute-start(bf16[8,288]{1,0:T(8,128)(2,1)S(1)} %get-tuple-element.153), channel_id=1, source_target_pairs={{0,4},{4,8},{8,12},{12,0},{1,5},{5,9},{9,13},{13,1},{2,6},{6,10},{... | collective-permute-start | bytes 13832 | tf_op jit(solution)/shard_map/ppermute | solution.py:499
  228.9 10.4 %collective-permute-start.41 = (bf16[2,48,768]{2,1,0:T(8,128)(2,1)S(1)}, bf16[2,48,768]{2,1,0:T(8,128)(2,1)S(1)}, u32[]{:S(2)}, u32[]{:S(2)}) collective-permute-start(bf16[2,48,768]{2,1,0:T(8,128)(2,1)S(1)} %pad_maximum_fusion.6), channel_id=1, source_target_pairs={{0,8},{4,12},{8,0},{12,4},{1,9},{5,13},{9,1},{13,5},{2,10},{6,14},... | collective-permute-start | bytes 442376 | tf_op jit(solution)/shard_map/ppermute | solution.py:499
  232.1 13.2 %collective-permute-start.34 = (bf16[2,64,768]{2,1,0:T(8,128)(2,1)S(1)}, bf16[2,64,768]{2,1,0:T(8,128)(2,1)S(1)}, u32[]{:S(2)}, u32[]{:S(2)}) collective-permute-start(bf16[2,64,768]{2,1,0:T(8,128)(2,1)S(1)} %pad_maximum_fusion.1), channel_id=1, source_target_pairs={{0,1},{1,2},{2,3},{3,0},{4,5},{5,6},{6,7},{7,4},{8,9},{9,10},{10,1... | collective-permute-start | bytes 589832 | tf_op jit(solution)/shard_map/ppermute | solution.py:499
  234.4 10.9 %collective-permute-start.35 = (bf16[2,64,768]{2,1,0:T(8,128)(2,1)S(1)}, bf16[2,64,768]{2,1,0:T(8,128)(2,1)S(1)}, u32[]{:S(2)}, u32[]{:S(2)}) collective-permute-start(bf16[2,64,768]{2,1,0:T(8,128)(2,1)S(1)} %pad_maximum_fusion.2), channel_id=1, source_target_pairs={{0,2},{1,3},{2,0},{3,1},{4,6},{5,7},{6,4},{7,5},{8,10},{9,11},{10,... | collective-permute-start | bytes 589832 | tf_op jit(solution)/shard_map/ppermute | solution.py:499
  (38 other events, 297.7 us)
